TPU v7x, 32 devices: a whole 2x2x4 slice. The times are simulated.
32 devices in a mesh: lat: 4 (over y, x), lon: 8 (over z, core).
Axes of the slice: x: 2, y: 2, z: 4, core: 2. Of those that a mesh axis runs over, the one named last changes fastest.
Arguments:
- feat_one: bfloat16 [64, 512, 256], P('lat', 'lon'), may hold values from -6 to 6
- feat_two: bfloat16 [64, 512, 256], P('lat', 'lon'), may hold values from -6 to 6
- context_in: bfloat16 [64, 512, 128], P('lat', 'lon'), may hold values from 0 to 2
- hidden_init: bfloat16 [64, 512, 128], P('lat', 'lon'), may hold values from -1 to 1
- corr_proj: bfloat16 [8, 128, 128], replicated, may hold values from -0.5 to 0.5
- input_conv: bfloat16 [2, 5, 256, 384], replicated, may hold values from -0.125 to 0.125
- state_zr: bfloat16 [2, 5, 128, 256], replicated, may hold values from -0.75 to 0.75
- state_q: bfloat16 [2, 5, 128, 128], replicated, may hold values from -0.75 to 0.75
- update_bias: float32 [2, 128], replicated, may hold values from -2 to 0
- gate_bias: float32 [2, 256], replicated, may hold values from -3 to 3
- blk_offset: int32 [4, 8, 12], P('lat', 'lon'), may hold values from -4 to 4, as said below
- blk_class: int32 [4, 8, 12], P('lat', 'lon'), may hold values from 0 to 7
- blk_count: int32 [4, 8], P('lat', 'lon'), may hold values from 1 to 12, as said below
Outputs:
- hidden: bfloat16 [64, 512, 128], P('lat', 'lon')
Inputs may be any that keep to these rules, and one draw needn't show every extreme that they name: `blk_offset`: offsets of panels along the closed longitude loop; bands nearer a pole reach farther, the bands at the poles up to 4 either way, and both ends are reached in every draw. Slots at or beyond blk_count are unused. `blk_count`: bands nearer a pole hold more live slots; some panel of the first band holds 12.
All inputs are finite; a program needn't handle non-finite values.
Results may differ from a plain program's by a relative error of at most 0.019.
Values may be sent and summed in bfloat16 or wider, within the bound.
A program may use at most 64 MiB of HBM per device.

v0:
```python
import jax
import jax.numpy as jnp
from jax import lax
from jax.sharding import PartitionSpec as P

POOLR = 8
POOLC = 16
RMAX = 4
ITERS = 4


def extended(block, sides, width, periodic):
    for axis, dim in sides:
        count = lax.axis_size(axis)
        forward = [(i, i + 1) for i in range(count - 1)]
        if periodic:
            forward.append((count - 1, 0))
        backward = [(target, source) for source, target in forward]
        low = lax.ppermute(
            lax.slice_in_dim(block, block.shape[dim] - width, None, axis=dim), axis, forward
        )
        high = lax.ppermute(lax.slice_in_dim(block, 0, width, axis=dim), axis, backward)
        block = jnp.concatenate([low, block, high], axis=dim)
    return block


def passed_along(value, axis, steps):
    count = lax.axis_size(axis)
    pairs = [(source, (source + steps) % count) for source in range(count)]
    return lax.ppermute(value, axis, pairs)


def rim_lon(values):
    return extended(values, (("lon", 1),), 2, True)


def rim_lat(values):
    return extended(values, (("lat", 0),), 2, False)


def conv_lon(values, weight):
    width = values.shape[1]
    padded = rim_lon(values)
    total = jnp.zeros((values.shape[0] * width, weight.shape[2]), jnp.float32)
    for tap in range(5):
        piece = padded[:, tap : tap + width].reshape(-1, values.shape[2])
        total = total + jnp.dot(piece, weight[tap], preferred_element_type=jnp.float32)
    return total


def conv_lat(values, weight):
    height = values.shape[0]
    padded = rim_lat(values)
    total = jnp.zeros((height * values.shape[1], weight.shape[2]), jnp.float32)
    for tap in range(5):
        piece = padded[tap : tap + height].reshape(-1, values.shape[2])
        total = total + jnp.dot(piece, weight[tap], preferred_element_type=jnp.float32)
    return total


def gru_pass(state, inputs, conv, zr_weight, q_weight, z_bias, gate_row, shape):
    hid = state.shape[1]
    state_bf = state.astype(jnp.bfloat16).reshape(shape)
    mixed = conv(state_bf, zr_weight)
    update = jax.nn.sigmoid(inputs[:, :hid] + mixed[:, :hid] + z_bias)
    reset = jax.nn.sigmoid(inputs[:, hid : 2 * hid] + mixed[:, hid:] + gate_row[:hid])
    reset_state = (reset * state).astype(jnp.bfloat16).reshape(shape)
    candidate = jnp.tanh(inputs[:, 2 * hid :] + conv(reset_state, q_weight) + gate_row[hid:])
    return (1.0 - update) * state + update * candidate


def local(
    feat_one,
    feat_two,
    context_in,
    hidden_init,
    corr_proj,
    input_conv,
    state_zr,
    state_q,
    update_bias,
    gate_bias,
    blk_offset,
    blk_class,
    blk_count,
):
    rows, cols, chans = feat_one.shape
    hid = hidden_init.shape[2]
    pool_rows = rows // POOLR
    pool_cols = cols // POOLC
    points = POOLR * POOLC
    grid = feat_two.reshape(POOLR, pool_rows, POOLC, pool_cols, chans)
    pooled = (jnp.sum(grid, axis=(1, 3), dtype=jnp.float32) / (pool_rows * pool_cols)).astype(
        jnp.bfloat16
    )
    pooled = pooled.reshape(points, chans)
    neighbours = []
    for step in range(-RMAX, RMAX + 1):
        if step == 0:
            neighbours.append(pooled)
        else:
            neighbours.append(passed_along(pooled, "lon", -step))
    table = jnp.stack(neighbours, axis=0)

    def pick(offset):
        return lax.dynamic_index_in_dim(table, offset + RMAX, 0, keepdims=False)

    queries = feat_one.reshape(rows * cols, chans)
    offsets = blk_offset[0, 0]
    classes = blk_class[0, 0]
    live = blk_count[0, 0]
    scale = chans ** (-0.5)

    def add_block(slot, total):
        keys = pick(offsets[slot])
        corr = (
            lax.dot_general(
                queries, keys, (((1,), (1,)), ((), ())), preferred_element_type=jnp.float32
            )
            * scale
        ).astype(jnp.bfloat16)
        proj = lax.dynamic_index_in_dim(corr_proj, classes[slot], 0, keepdims=False)
        return total + jnp.dot(corr, proj, preferred_element_type=jnp.float32)

    motion_sum = lax.fori_loop(0, live, add_block, jnp.zeros((rows * cols, hid), jnp.float32))
    motion = jnp.maximum(motion_sum, 0.0).astype(jnp.bfloat16).reshape(rows, cols, hid)
    joined = jnp.concatenate([context_in, motion], axis=2)
    x_lon = conv_lon(joined, input_conv[0])
    x_lat = conv_lat(joined, input_conv[1])
    shape = (rows, cols, hid)
    state = hidden_init.astype(jnp.float32).reshape(-1, hid)
    for step in range(ITERS):
        state = gru_pass(
            state, x_lon, conv_lon, state_zr[0], state_q[0], update_bias[0], gate_bias[0], shape
        )
        state = gru_pass(
            state, x_lat, conv_lat, state_zr[1], state_q[1], update_bias[1], gate_bias[1], shape
        )
    return state.astype(jnp.bfloat16).reshape(shape)


def solution(mesh):
    placed = (
        P("lat", "lon", None),
        P("lat", "lon", None),
        P("lat", "lon", None),
        P("lat", "lon", None),
        P(),
        P(),
        P(),
        P(),
        P(),
        P(),
        P("lat", "lon", None),
        P("lat", "lon", None),
        P("lat", "lon"),
    )
    return jax.shard_map(
        local, mesh=mesh, in_specs=placed, out_specs=P("lat", "lon", None), check_vma=False
    )
```

profile of v0, /device:TPU:0, one launch (start us, length us, event | category | flops | bytes accessed | tf_op | source)
XLA Modules:
  0.0 258.8 jit_solution(7499184673778554535)
XLA Ops:
  0.0 1.3 reshape.484
  1.8 4.1 %collective-permute-start = (bf16[128,256]{1,0:T(8,128)(2,1)S(1)}, bf16[128,256]{1,0:T(8,128)(2,1)S(1)}, u32[]{:S(2)}, u32[]{:S(2)}) collective-permute-start(bf16[128,256]{1,0:T(8,128)(2,1)S(1)} %bitcast.573), channel_id=1, source_target_pairs={{0,4},{1,5},{2,6},{3,7},{4,0},{5,1},{6,2},{7,3},{8,12},{9,13},{10,... | collective-permute-start | bytes 196616 | tf_op jit(solution)/shard_map/ppermute | solution.py:30
  7.7 6.3 %collective-permute-done.11 = bf16[16,2,128]{2,1,0:T(2,128)(2,1)S(1)} collective-permute-done((bf16[16,2,128]{2,1,0:T(2,128)(2,1)S(1)}, bf16[16,2,128]{2,1,0:T(2,128)(2,1)S(1)}, u32[]{:S(2)}, u32[]{:S(2)}) %collective-permute-start.11) | collective-permute-done | bytes 8224 | tf_op jit(solution)/shard_map/ppermute | solution.py:19
  15.4 3.5 %collective-permute-start.4 = (bf16[128,256]{1,0:T(8,128)(2,1)S(1)}, bf16[128,256]{1,0:T(8,128)(2,1)S(1)}, u32[]{:S(2)}, u32[]{:S(2)}) collective-permute-start(bf16[128,256]{1,0:T(8,128)(2,1)S(1)} %bitcast.577), channel_id=1, source_target_pairs={{0,7},{1,0},{2,1},{3,2},{4,3},{5,4},{6,5},{7,6},{8,15},{9,8},{10,9... | collective-permute-start | bytes 196616 | tf_op jit(solution)/shard_map/ppermute | solution.py:30
  21.4 4.2 %collective-permute-done.5 = bf16[128,256]{1,0:T(8,128)(2,1)S(1)} collective-permute-done((bf16[128,256]{1,0:T(8,128)(2,1)S(1)}, bf16[128,256]{1,0:T(8,128)(2,1)S(1)}, u32[]{:S(2)}, u32[]{:S(2)}) %collective-permute-start.5) | collective-permute-done | bytes 65568 | tf_op jit(solution)/shard_map/ppermute | solution.py:30
  26.6 67.9 %while.12 = (s32[]{:T(128)}, f32[1024,128]{1,0:T(8,128)S(1)}, s32[]{:T(128)}, s32[12]{0:T(128)S(1)}, bf16[9,128,256]{2,1,0:T(8,128)(2,1)}, /*index=5*/bf16[1024,...) while((s32[]{:T(128)}, f32[1024,128]{1,0:T(8,128)S(1)}, ...), condition=%wide.region_2.3_spmd, body=%wide.region_1.2_spmd.sunk | while | flops 101056520 | bytes 1671447 | solution.py:125
  32.0 1.4 convolution_add_fusion.65
  38.7 1.4 convolution_add_fusion.65
  45.4 1.4 convolution_add_fusion.65
  52.1 1.4 convolution_add_fusion.65
  58.8 1.4 convolution_add_fusion.65
  65.6 1.4 convolution_add_fusion.65
  72.3 1.4 convolution_add_fusion.65
  79.0 1.4 convolution_add_fusion.65
  85.7 1.4 convolution_add_fusion.65
  92.4 1.4 convolution_add_fusion.65
  94.6 9.8 %collective-permute-start.10 = (bf16[16,2,256]{2,1,0:T(2,128)(2,1)S(1)}, bf16[16,2,256]{2,1,0:T(2,128)(2,1)S(1)}, u32[]{:S(2)}, u32[]{:S(2)}) collective-permute-start(bf16[16,2,256]{2,1,0:T(2,128)(2,1)S(1)} %get-tuple-element.141), channel_id=1, source_target_pairs={{1,0},{2,1},{3,2},{4,3},{5,4},{6,5},{7,6},{0,7},{9,8},{10,9},{11,1... | collective-permute-start | bytes 49160 | tf_op jit(solution)/shard_map/ppermute | solution.py:22
  104.4 4.5 %collective-permute-start.9 = (bf16[16,2,256]{2,1,0:T(2,128)(2,1)S(1)}, bf16[16,2,256]{2,1,0:T(2,128)(2,1)S(1)}, u32[]{:S(2)}, u32[]{:S(2)}) collective-permute-start(bf16[16,2,256]{2,1,0:T(2,128)(2,1)S(1)} %get-tuple-element.140), channel_id=1, source_target_pairs={{0,1},{1,2},{2,3},{3,4},{4,5},{5,6},{6,7},{7,0},{8,9},{9,10},{10,1... | collective-permute-start | bytes 49160 | tf_op jit(solution)/shard_map/ppermute | solution.py:19
  108.9 1.4 fusion.143
  114.3 1.8 collective-permute-start.13
  116.0 1.8 collective-permute-start.14
  123.4 4.5 %collective-permute-start.7 = (bf16[2,64,256]{2,1,0:T(8,128)(2,1)S(1)}, bf16[2,64,256]{2,1,0:T(8,128)(2,1)S(1)}, u32[]{:S(2)}, u32[]{:S(2)}) collective-permute-start(bf16[2,64,256]{2,1,0:T(8,128)(2,1)S(1)} %get-tuple-element.136), channel_id=1, source_target_pairs={{0,8},{8,16},{16,24},{1,9},{9,17},{17,25},{2,10},{10,18},{18,26},{... | collective-permute-start | bytes 196616 | tf_op jit(solution)/shard_map/ppermute | solution.py:19
  130.8 10.1 %collective-permute-done.8 = bf16[2,64,256]{2,1,0:T(8,128)(2,1)S(1)} collective-permute-done((bf16[2,64,256]{2,1,0:T(8,128)(2,1)S(1)}, bf16[2,64,256]{2,1,0:T(8,128)(2,1)S(1)}, u32[]{:S(2)}, u32[]{:S(2)}) %collective-permute-start.8) | collective-permute-done | bytes 65568 | tf_op jit(solution)/shard_map/ppermute | solution.py:22
  143.2 4.8 %collective-permute-start.17 = (bf16[2,64,128]{2,1,0:T(8,128)(2,1)S(1)}, bf16[2,64,128]{2,1,0:T(8,128)(2,1)S(1)}, u32[]{:S(2)}, u32[]{:S(2)}) collective-permute-start(bf16[2,64,128]{2,1,0:T(8,128)(2,1)S(1)} %bitcast.598), channel_id=1, source_target_pairs={{0,8},{8,16},{16,24},{1,9},{9,17},{17,25},{2,10},{10,18},{18,26},{... | collective-permute-start | bytes 98312 | tf_op jit(solution)/shard_map/ppermute | solution.py:19
  148.1 1.5 collective-permute-start.18
  149.7 4.2 %collective-permute-done.18 = bf16[2,64,128]{2,1,0:T(8,128)(2,1)S(1)} collective-permute-done((bf16[2,64,128]{2,1,0:T(8,128)(2,1)S(1)}, bf16[2,64,128]{2,1,0:T(8,128)(2,1)S(1)}, u32[]{:S(2)}, u32[]{:S(2)}) %collective-permute-start.18) | collective-permute-done | bytes 32800 | tf_op jit(solution)/shard_map/ppermute | solution.py:22
  155.3 3.5 %collective-permute-start.20 = (bf16[16,2,128]{2,1,0:T(2,128)(2,1)S(1)}, bf16[16,2,128]{2,1,0:T(2,128)(2,1)S(1)}, u32[]{:S(2)}, u32[]{:S(2)}) collective-permute-start(bf16[16,2,128]{2,1,0:T(2,128)(2,1)S(1)} %get-tuple-element.252), channel_id=1, source_target_pairs={{1,0},{2,1},{3,2},{4,3},{5,4},{6,5},{7,6},{0,7},{9,8},{10,9},{11,1... | collective-permute-start | bytes 24584 | tf_op jit(solution)/shard_map/ppermute | solution.py:22
  158.8 1.3 collective-permute-done.19
  162.2 3.6 %collective-permute-start.22 = (bf16[16,2,128]{2,1,0:T(2,128)(2,1)S(1)}, bf16[16,2,128]{2,1,0:T(2,128)(2,1)S(1)}, u32[]{:S(2)}, u32[]{:S(2)}) collective-permute-start(bf16[16,2,128]{2,1,0:T(2,128)(2,1)S(1)} %get-tuple-element.248), channel_id=1, source_target_pairs={{1,0},{2,1},{3,2},{4,3},{5,4},{6,5},{7,6},{0,7},{9,8},{10,9},{11,1... | collective-permute-start | bytes 24584 | tf_op jit(solution)/shard_map/ppermute | solution.py:22
  168.6 3.9 %collective-permute-start.23 = (bf16[2,64,128]{2,1,0:T(8,128)(2,1)S(1)}, bf16[2,64,128]{2,1,0:T(8,128)(2,1)S(1)}, u32[]{:S(2)}, u32[]{:S(2)}) collective-permute-start(bf16[2,64,128]{2,1,0:T(8,128)(2,1)S(1)} %bitcast.599), channel_id=1, source_target_pairs={{0,8},{8,16},{16,24},{1,9},{9,17},{17,25},{2,10},{10,18},{18,26},{... | collective-permute-start | bytes 98312 | tf_op jit(solution)/shard_map/ppermute | solution.py:19
  174.1 4.2 %collective-permute-done.24 = bf16[2,64,128]{2,1,0:T(8,128)(2,1)S(1)} collective-permute-done((bf16[2,64,128]{2,1,0:T(8,128)(2,1)S(1)}, bf16[2,64,128]{2,1,0:T(8,128)(2,1)S(1)}, u32[]{:S(2)}, u32[]{:S(2)}) %collective-permute-start.24) | collective-permute-done | bytes 32800 | tf_op jit(solution)/shard_map/ppermute | solution.py:22
  180.0 3.1 %collective-permute-start.25 = (bf16[2,64,128]{2,1,0:T(8,128)(2,1)S(1)}, bf16[2,64,128]{2,1,0:T(8,128)(2,1)S(1)}, u32[]{:S(2)}, u32[]{:S(2)}) collective-permute-start(bf16[2,64,128]{2,1,0:T(8,128)(2,1)S(1)} %bitcast.600), channel_id=1, source_target_pairs={{0,8},{8,16},{16,24},{1,9},{9,17},{17,25},{2,10},{10,18},{18,26},{... | collective-permute-start | bytes 98312 | tf_op jit(solution)/shard_map/ppermute | solution.py:19
  184.6 4.2 %collective-permute-done.26 = bf16[2,64,128]{2,1,0:T(8,128)(2,1)S(1)} collective-permute-done((bf16[2,64,128]{2,1,0:T(8,128)(2,1)S(1)}, bf16[2,64,128]{2,1,0:T(8,128)(2,1)S(1)}, u32[]{:S(2)}, u32[]{:S(2)}) %collective-permute-start.26) | collective-permute-done | bytes 32800 | tf_op jit(solution)/shard_map/ppermute | solution.py:22
  190.3 3.5 %collective-permute-start.28 = (bf16[16,2,128]{2,1,0:T(2,128)(2,1)S(1)}, bf16[16,2,128]{2,1,0:T(2,128)(2,1)S(1)}, u32[]{:S(2)}, u32[]{:S(2)}) collective-permute-start(bf16[16,2,128]{2,1,0:T(2,128)(2,1)S(1)} %get-tuple-element.236), channel_id=1, source_target_pairs={{1,0},{2,1},{3,2},{4,3},{5,4},{6,5},{7,6},{0,7},{9,8},{10,9},{11,1... | collective-permute-start | bytes 24584 | tf_op jit(solution)/shard_map/ppermute | solution.py:22
  193.8 1.3 collective-permute-done.27
  197.2 3.6 %collective-permute-start.30 = (bf16[16,2,128]{2,1,0:T(2,128)(2,1)S(1)}, bf16[16,2,128]{2,1,0:T(2,128)(2,1)S(1)}, u32[]{:S(2)}, u32[]{:S(2)}) collective-permute-start(bf16[16,2,128]{2,1,0:T(2,128)(2,1)S(1)} %get-tuple-element.232), channel_id=1, source_target_pairs={{1,0},{2,1},{3,2},{4,3},{5,4},{6,5},{7,6},{0,7},{9,8},{10,9},{11,1... | collective-permute-start | bytes 24584 | tf_op jit(solution)/shard_map/ppermute | solution.py:22
  200.7 1.3 collective-permute-done.29
  203.6 2.8 %collective-permute-start.31 = (bf16[2,64,128]{2,1,0:T(8,128)(2,1)S(1)}, bf16[2,64,128]{2,1,0:T(8,128)(2,1)S(1)}, u32[]{:S(2)}, u32[]{:S(2)}) collective-permute-start(bf16[2,64,128]{2,1,0:T(8,128)(2,1)S(1)} %bitcast.601), channel_id=1, source_target_pairs={{0,8},{8,16},{16,24},{1,9},{9,17},{17,25},{2,10},{10,18},{18,26},{... | collective-permute-start | bytes 98312 | tf_op jit(solution)/shard_map/ppermute | solution.py:19
  208.0 4.2 %collective-permute-done.32 = bf16[2,64,128]{2,1,0:T(8,128)(2,1)S(1)} collective-permute-done((bf16[2,64,128]{2,1,0:T(8,128)(2,1)S(1)}, bf16[2,64,128]{2,1,0:T(8,128)(2,1)S(1)}, u32[]{:S(2)}, u32[]{:S(2)}) %collective-permute-start.32) | collective-permute-done | bytes 32800 | tf_op jit(solution)/shard_map/ppermute | solution.py:22
  213.9 3.1 %collective-permute-start.33 = (bf16[2,64,128]{2,1,0:T(8,128)(2,1)S(1)}, bf16[2,64,128]{2,1,0:T(8,128)(2,1)S(1)}, u32[]{:S(2)}, u32[]{:S(2)}) collective-permute-start(bf16[2,64,128]{2,1,0:T(8,128)(2,1)S(1)} %bitcast.602), channel_id=1, source_target_pairs={{0,8},{8,16},{16,24},{1,9},{9,17},{17,25},{2,10},{10,18},{18,26},{... | collective-permute-start | bytes 98312 | tf_op jit(solution)/shard_map/ppermute | solution.py:19
  218.6 4.2 %collective-permute-done.34 = bf16[2,64,128]{2,1,0:T(8,128)(2,1)S(1)} collective-permute-done((bf16[2,64,128]{2,1,0:T(8,128)(2,1)S(1)}, bf16[2,64,128]{2,1,0:T(8,128)(2,1)S(1)}, u32[]{:S(2)}, u32[]{:S(2)}) %collective-permute-start.34) | collective-permute-done | bytes 32800 | tf_op jit(solution)/shard_map/ppermute | solution.py:22
  224.2 3.5 %collective-permute-start.36 = (bf16[16,2,128]{2,1,0:T(2,128)(2,1)S(1)}, bf16[16,2,128]{2,1,0:T(2,128)(2,1)S(1)}, u32[]{:S(2)}, u32[]{:S(2)}) collective-permute-start(bf16[16,2,128]{2,1,0:T(2,128)(2,1)S(1)} %get-tuple-element.220), channel_id=1, source_target_pairs={{1,0},{2,1},{3,2},{4,3},{5,4},{6,5},{7,6},{0,7},{9,8},{10,9},{11,1... | collective-permute-start | bytes 24584 | tf_op jit(solution)/shard_map/ppermute | solution.py:22
  227.8 1.3 collective-permute-done.35
  231.1 3.6 %collective-permute-start.38 = (bf16[16,2,128]{2,1,0:T(2,128)(2,1)S(1)}, bf16[16,2,128]{2,1,0:T(2,128)(2,1)S(1)}, u32[]{:S(2)}, u32[]{:S(2)}) collective-permute-start(bf16[16,2,128]{2,1,0:T(2,128)(2,1)S(1)} %get-tuple-element.216), channel_id=1, source_target_pairs={{1,0},{2,1},{3,2},{4,3},{5,4},{6,5},{7,6},{0,7},{9,8},{10,9},{11,1... | collective-permute-start | bytes 24584 | tf_op jit(solution)/shard_map/ppermute | solution.py:22
  237.6 2.8 %collective-permute-start.39 = (bf16[2,64,128]{2,1,0:T(8,128)(2,1)S(1)}, bf16[2,64,128]{2,1,0:T(8,128)(2,1)S(1)}, u32[]{:S(2)}, u32[]{:S(2)}) collective-permute-start(bf16[2,64,128]{2,1,0:T(8,128)(2,1)S(1)} %bitcast.603), channel_id=1, source_target_pairs={{0,8},{8,16},{16,24},{1,9},{9,17},{17,25},{2,10},{10,18},{18,26},{... | collective-permute-start | bytes 98312 | tf_op jit(solution)/shard_map/ppermute | solution.py:19
  242.0 4.2 %collective-permute-done.40 = bf16[2,64,128]{2,1,0:T(8,128)(2,1)S(1)} collective-permute-done((bf16[2,64,128]{2,1,0:T(8,128)(2,1)S(1)}, bf16[2,64,128]{2,1,0:T(8,128)(2,1)S(1)}, u32[]{:S(2)}, u32[]{:S(2)}) %collective-permute-start.40) | collective-permute-done | bytes 32800 | tf_op jit(solution)/shard_map/ppermute | solution.py:22
  247.9 3.1 %collective-permute-start.41 = (bf16[2,64,128]{2,1,0:T(8,128)(2,1)S(1)}, bf16[2,64,128]{2,1,0:T(8,128)(2,1)S(1)}, u32[]{:S(2)}, u32[]{:S(2)}) collective-permute-start(bf16[2,64,128]{2,1,0:T(8,128)(2,1)S(1)} %bitcast.604), channel_id=1, source_target_pairs={{0,8},{8,16},{16,24},{1,9},{9,17},{17,25},{2,10},{10,18},{18,26},{... | collective-permute-start | bytes 98312 | tf_op jit(solution)/shard_map/ppermute | solution.py:19
  252.6 4.2 %collective-permute-done.42 = bf16[2,64,128]{2,1,0:T(8,128)(2,1)S(1)} collective-permute-done((bf16[2,64,128]{2,1,0:T(8,128)(2,1)S(1)}, bf16[2,64,128]{2,1,0:T(8,128)(2,1)S(1)}, u32[]{:S(2)}, u32[]{:S(2)}) %collective-permute-start.42) | collective-permute-done | bytes 32800 | tf_op jit(solution)/shard_map/ppermute | solution.py:22
  (244 shorter events, 68.1 us)
Async XLA Ops:
  0.0 7.6 %copy-start.4 = (bf16[16,64,128]{2,1,0:T(8,128)(2,1)S(1)}, bf16[16,64,128]{2,1,0:T(8,128)(2,1)}, u32[]{:S(2)}) copy-start(bf16[16,64,128]{2,1,0:T(8,128)(2,1)} %param.18) | copy-start | bytes 786436
  0.0 7.7 %copy-start.8 = (f32[2,128]{1,0:T(2,128)S(1)}, f32[2,128]{1,0:T(2,128)}, u32[]{:S(2)}) copy-start(f32[2,128]{1,0:T(2,128)} %param.23) | copy-start | bytes 3076
  0.0 7.7 %copy-start.7 = (f32[2,256]{1,0:T(2,128)S(1)}, f32[2,256]{1,0:T(2,128)}, u32[]{:S(2)}) copy-start(f32[2,256]{1,0:T(2,128)} %param.24) | copy-start | bytes 6148
  1.3 17.7 %copy-start.1 = (bf16[2,5,128,256]{3,2,1,0:T(8,128)(2,1)S(1)}, bf16[2,5,128,256]{3,2,1,0:T(8,128)(2,1)}, u32[]{:S(2)}) copy-start(bf16[2,5,128,256]{3,2,1,0:T(8,128)(2,1)} %param.21) | copy-start | bytes 1966084
  1.8 18.8 %collective-permute-start = (bf16[128,256]{1,0:T(8,128)(2,1)S(1)}, bf16[128,256]{1,0:T(8,128)(2,1)S(1)}, u32[]{:S(2)}, u32[]{:S(2)}) collective-permute-start(bf16[128,256]{1,0:T(8,128)(2,1)S(1)} %bitcast.573), channel_id=1, source_target_pairs={{0,4},{1,5},{2,6},{3,7},{4,0},{5,1},{6,2},{7,3},{8,12},{9,13},{10,... | collective-permute-start | bytes 196616 | tf_op jit(solution)/shard_map/ppermute | solution.py:30
  5.9 15.4 %collective-permute-start.1 = (bf16[128,256]{1,0:T(8,128)(2,1)S(1)}, bf16[128,256]{1,0:T(8,128)(2,1)S(1)}, u32[]{:S(2)}, u32[]{:S(2)}) collective-permute-start(bf16[128,256]{1,0:T(8,128)(2,1)S(1)} %bitcast.574), channel_id=1, source_target_pairs={{0,3},{1,4},{2,5},{3,6},{4,7},{5,0},{6,1},{7,2},{8,11},{9,12},{10,... | collective-permute-start | bytes 196616 | tf_op jit(solution)/shard_map/ppermute | solution.py:30
  6.6 14.7 %collective-permute-start.2 = (bf16[128,256]{1,0:T(8,128)(2,1)S(1)}, bf16[128,256]{1,0:T(8,128)(2,1)S(1)}, u32[]{:S(2)}, u32[]{:S(2)}) collective-permute-start(bf16[128,256]{1,0:T(8,128)(2,1)S(1)} %bitcast.575), channel_id=1, source_target_pairs={{0,2},{1,3},{2,4},{3,5},{4,6},{5,7},{6,0},{7,1},{8,10},{9,11},{10,... | collective-permute-start | bytes 196616 | tf_op jit(solution)/shard_map/ppermute | solution.py:30
  7.4 13.9 %collective-permute-start.3 = (bf16[128,256]{1,0:T(8,128)(2,1)S(1)}, bf16[128,256]{1,0:T(8,128)(2,1)S(1)}, u32[]{:S(2)}, u32[]{:S(2)}) collective-permute-start(bf16[128,256]{1,0:T(8,128)(2,1)S(1)} %bitcast.576), channel_id=1, source_target_pairs={{0,1},{1,2},{2,3},{3,4},{4,5},{5,6},{6,7},{7,0},{8,9},{9,10},{10,1... | collective-permute-start | bytes 196616 | tf_op jit(solution)/shard_map/ppermute | solution.py:30
  7.6 6.4 %collective-permute-start.11 = (bf16[16,2,128]{2,1,0:T(2,128)(2,1)S(1)}, bf16[16,2,128]{2,1,0:T(2,128)(2,1)S(1)}, u32[]{:S(2)}, u32[]{:S(2)}) collective-permute-start(bf16[16,2,128]{2,1,0:T(2,128)(2,1)S(1)} %get-tuple-element.267), channel_id=1, source_target_pairs={{0,1},{1,2},{2,3},{3,4},{4,5},{5,6},{6,7},{7,0},{8,9},{9,10},{10,1... | collective-permute-start | bytes 24584 | tf_op jit(solution)/shard_map/ppermute | solution.py:19
  14.0 1.4 collective-permute-start.12
  15.4 6.0 %collective-permute-start.4 = (bf16[128,256]{1,0:T(8,128)(2,1)S(1)}, bf16[128,256]{1,0:T(8,128)(2,1)S(1)}, u32[]{:S(2)}, u32[]{:S(2)}) collective-permute-start(bf16[128,256]{1,0:T(8,128)(2,1)S(1)} %bitcast.577), channel_id=1, source_target_pairs={{0,7},{1,0},{2,1},{3,2},{4,3},{5,4},{6,5},{7,6},{8,15},{9,8},{10,9... | collective-permute-start | bytes 196616 | tf_op jit(solution)/shard_map/ppermute | solution.py:30
  20.5 5.1 %collective-permute-start.5 = (bf16[128,256]{1,0:T(8,128)(2,1)S(1)}, bf16[128,256]{1,0:T(8,128)(2,1)S(1)}, u32[]{:S(2)}, u32[]{:S(2)}) collective-permute-start(bf16[128,256]{1,0:T(8,128)(2,1)S(1)} %bitcast.578), channel_id=1, source_target_pairs={{0,6},{1,7},{2,0},{3,1},{4,2},{5,3},{6,4},{7,5},{8,14},{9,15},{10,... | collective-permute-start | bytes 196616 | tf_op jit(solution)/shard_map/ppermute | solution.py:30
  21.3 4.5 %collective-permute-start.6 = (bf16[128,256]{1,0:T(8,128)(2,1)S(1)}, bf16[128,256]{1,0:T(8,128)(2,1)S(1)}, u32[]{:S(2)}, u32[]{:S(2)}) collective-permute-start(bf16[128,256]{1,0:T(8,128)(2,1)S(1)} %bitcast.579), channel_id=1, source_target_pairs={{0,5},{1,6},{2,7},{3,0},{4,1},{5,2},{6,3},{7,4},{8,13},{9,14},{10,... | collective-permute-start | bytes 196616 | tf_op jit(solution)/shard_map/ppermute | solution.py:30
  26.6 67.9 %copy-start.2 = (bf16[16,64,128]{2,1,0:T(8,128)(2,1)S(1)}, bf16[16,64,128]{2,1,0:T(8,128)(2,1)}, u32[]{:S(2)}) copy-start(bf16[16,64,128]{2,1,0:T(8,128)(2,1)} %param.17) | copy-start | bytes 786436
  94.6 15.7 %collective-permute-start.10 = (bf16[16,2,256]{2,1,0:T(2,128)(2,1)S(1)}, bf16[16,2,256]{2,1,0:T(2,128)(2,1)S(1)}, u32[]{:S(2)}, u32[]{:S(2)}) collective-permute-start(bf16[16,2,256]{2,1,0:T(2,128)(2,1)S(1)} %get-tuple-element.141), channel_id=1, source_target_pairs={{1,0},{2,1},{3,2},{4,3},{5,4},{6,5},{7,6},{0,7},{9,8},{10,9},{11,1... | collective-permute-start | bytes 49160 | tf_op jit(solution)/shard_map/ppermute | solution.py:22
  104.4 5.9 %collective-permute-start.9 = (bf16[16,2,256]{2,1,0:T(2,128)(2,1)S(1)}, bf16[16,2,256]{2,1,0:T(2,128)(2,1)S(1)}, u32[]{:S(2)}, u32[]{:S(2)}) collective-permute-start(bf16[16,2,256]{2,1,0:T(2,128)(2,1)S(1)} %get-tuple-element.140), channel_id=1, source_target_pairs={{0,1},{1,2},{2,3},{3,4},{4,5},{5,6},{6,7},{7,0},{8,9},{9,10},{10,1... | collective-permute-start | bytes 49160 | tf_op jit(solution)/shard_map/ppermute | solution.py:19
  114.3 4.9 %collective-permute-start.13 = (bf16[16,2,128]{2,1,0:T(2,128)(2,1)S(1)}, bf16[16,2,128]{2,1,0:T(2,128)(2,1)S(1)}, u32[]{:S(2)}, u32[]{:S(2)}) collective-permute-start(bf16[16,2,128]{2,1,0:T(2,128)(2,1)S(1)} %get-tuple-element.265), channel_id=1, source_target_pairs={{0,1},{1,2},{2,3},{3,4},{4,5},{5,6},{6,7},{7,0},{8,9},{9,10},{10,1... | collective-permute-start | bytes 24584 | tf_op jit(solution)/shard_map/ppermute | solution.py:19
  116.0 3.2 %collective-permute-start.14 = (bf16[16,2,128]{2,1,0:T(2,128)(2,1)S(1)}, bf16[16,2,128]{2,1,0:T(2,128)(2,1)S(1)}, u32[]{:S(2)}, u32[]{:S(2)}) collective-permute-start(bf16[16,2,128]{2,1,0:T(2,128)(2,1)S(1)} %get-tuple-element.264), channel_id=1, source_target_pairs={{1,0},{2,1},{3,2},{4,3},{5,4},{6,5},{7,6},{0,7},{9,8},{10,9},{11,1... | collective-permute-start | bytes 24584 | tf_op jit(solution)/shard_map/ppermute | solution.py:22
  120.8 8.5 %collective-permute-start.15 = (bf16[2,64,128]{2,1,0:T(8,128)(2,1)S(1)}, bf16[2,64,128]{2,1,0:T(8,128)(2,1)S(1)}, u32[]{:S(2)}, u32[]{:S(2)}) collective-permute-start(bf16[2,64,128]{2,1,0:T(8,128)(2,1)S(1)} %bitcast.590), channel_id=1, source_target_pairs={{0,8},{8,16},{16,24},{1,9},{9,17},{17,25},{2,10},{10,18},{18,26},{... | collective-permute-start | bytes 98312 | tf_op jit(solution)/shard_map/ppermute | solution.py:19
  122.1 7.2 %collective-permute-start.16 = (bf16[2,64,128]{2,1,0:T(8,128)(2,1)S(1)}, bf16[2,64,128]{2,1,0:T(8,128)(2,1)S(1)}, u32[]{:S(2)}, u32[]{:S(2)}) collective-permute-start(bf16[2,64,128]{2,1,0:T(8,128)(2,1)S(1)} %bitcast.589), channel_id=1, source_target_pairs={{8,0},{16,8},{24,16},{9,1},{17,9},{25,17},{10,2},{18,10},{26,18},{... | collective-permute-start | bytes 98312 | tf_op jit(solution)/shard_map/ppermute | solution.py:22
  123.4 7.4 %collective-permute-start.7 = (bf16[2,64,256]{2,1,0:T(8,128)(2,1)S(1)}, bf16[2,64,256]{2,1,0:T(8,128)(2,1)S(1)}, u32[]{:S(2)}, u32[]{:S(2)}) collective-permute-start(bf16[2,64,256]{2,1,0:T(8,128)(2,1)S(1)} %get-tuple-element.136), channel_id=1, source_target_pairs={{0,8},{8,16},{16,24},{1,9},{9,17},{17,25},{2,10},{10,18},{18,26},{... | collective-permute-start | bytes 196616 | tf_op jit(solution)/shard_map/ppermute | solution.py:19
  128.0 13.0 %collective-permute-start.8 = (bf16[2,64,256]{2,1,0:T(8,128)(2,1)S(1)}, bf16[2,64,256]{2,1,0:T(8,128)(2,1)S(1)}, u32[]{:S(2)}, u32[]{:S(2)}) collective-permute-start(bf16[2,64,256]{2,1,0:T(8,128)(2,1)S(1)} %get-tuple-element.137), channel_id=1, source_target_pairs={{8,0},{16,8},{24,16},{9,1},{17,9},{25,17},{10,2},{18,10},{26,18},{... | collective-permute-start | bytes 196616 | tf_op jit(solution)/shard_map/ppermute | solution.py:22
  143.2 6.4 %collective-permute-start.17 = (bf16[2,64,128]{2,1,0:T(8,128)(2,1)S(1)}, bf16[2,64,128]{2,1,0:T(8,128)(2,1)S(1)}, u32[]{:S(2)}, u32[]{:S(2)}) collective-permute-start(bf16[2,64,128]{2,1,0:T(8,128)(2,1)S(1)} %bitcast.598), channel_id=1, source_target_pairs={{0,8},{8,16},{16,24},{1,9},{9,17},{17,25},{2,10},{10,18},{18,26},{... | collective-permute-start | bytes 98312 | tf_op jit(solution)/shard_map/ppermute | solution.py:19
  148.1 5.8 %collective-permute-start.18 = (bf16[2,64,128]{2,1,0:T(8,128)(2,1)S(1)}, bf16[2,64,128]{2,1,0:T(8,128)(2,1)S(1)}, u32[]{:S(2)}, u32[]{:S(2)}) collective-permute-start(bf16[2,64,128]{2,1,0:T(8,128)(2,1)S(1)} %bitcast.591), channel_id=1, source_target_pairs={{8,0},{16,8},{24,16},{9,1},{17,9},{25,17},{10,2},{18,10},{26,18},{... | collective-permute-start | bytes 98312 | tf_op jit(solution)/shard_map/ppermute | solution.py:22
  155.2 4.9 %collective-permute-start.19 = (bf16[16,2,128]{2,1,0:T(2,128)(2,1)S(1)}, bf16[16,2,128]{2,1,0:T(2,128)(2,1)S(1)}, u32[]{:S(2)}, u32[]{:S(2)}) collective-permute-start(bf16[16,2,128]{2,1,0:T(2,128)(2,1)S(1)} %get-tuple-element.253), channel_id=1, source_target_pairs={{0,1},{1,2},{2,3},{3,4},{4,5},{5,6},{6,7},{7,0},{8,9},{9,10},{10,1... | collective-permute-start | bytes 24584 | tf_op jit(solution)/shard_map/ppermute | solution.py:19
  155.3 4.9 %collective-permute-start.20 = (bf16[16,2,128]{2,1,0:T(2,128)(2,1)S(1)}, bf16[16,2,128]{2,1,0:T(2,128)(2,1)S(1)}, u32[]{:S(2)}, u32[]{:S(2)}) collective-permute-start(bf16[16,2,128]{2,1,0:T(2,128)(2,1)S(1)} %get-tuple-element.252), channel_id=1, source_target_pairs={{1,0},{2,1},{3,2},{4,3},{5,4},{6,5},{7,6},{0,7},{9,8},{10,9},{11,1... | collective-permute-start | bytes 24584 | tf_op jit(solution)/shard_map/ppermute | solution.py:22
  162.1 4.9 %collective-permute-start.21 = (bf16[16,2,128]{2,1,0:T(2,128)(2,1)S(1)}, bf16[16,2,128]{2,1,0:T(2,128)(2,1)S(1)}, u32[]{:S(2)}, u32[]{:S(2)}) collective-permute-start(bf16[16,2,128]{2,1,0:T(2,128)(2,1)S(1)} %get-tuple-element.249), channel_id=1, source_target_pairs={{0,1},{1,2},{2,3},{3,4},{4,5},{5,6},{6,7},{7,0},{8,9},{9,10},{10,1... | collective-permute-start | bytes 24584 | tf_op jit(solution)/shard_map/ppermute | solution.py:19
  162.2 4.9 %collective-permute-start.22 = (bf16[16,2,128]{2,1,0:T(2,128)(2,1)S(1)}, bf16[16,2,128]{2,1,0:T(2,128)(2,1)S(1)}, u32[]{:S(2)}, u32[]{:S(2)}) collective-permute-start(bf16[16,2,128]{2,1,0:T(2,128)(2,1)S(1)} %get-tuple-element.248), channel_id=1, source_target_pairs={{1,0},{2,1},{3,2},{4,3},{5,4},{6,5},{7,6},{0,7},{9,8},{10,9},{11,1... | collective-permute-start | bytes 24584 | tf_op jit(solution)/shard_map/ppermute | solution.py:22
  168.6 5.5 %collective-permute-start.23 = (bf16[2,64,128]{2,1,0:T(8,128)(2,1)S(1)}, bf16[2,64,128]{2,1,0:T(8,128)(2,1)S(1)}, u32[]{:S(2)}, u32[]{:S(2)}) collective-permute-start(bf16[2,64,128]{2,1,0:T(8,128)(2,1)S(1)} %bitcast.599), channel_id=1, source_target_pairs={{0,8},{8,16},{16,24},{1,9},{9,17},{17,25},{2,10},{10,18},{18,26},{... | collective-permute-start | bytes 98312 | tf_op jit(solution)/shard_map/ppermute | solution.py:19
  172.5 5.8 %collective-permute-start.24 = (bf16[2,64,128]{2,1,0:T(8,128)(2,1)S(1)}, bf16[2,64,128]{2,1,0:T(8,128)(2,1)S(1)}, u32[]{:S(2)}, u32[]{:S(2)}) collective-permute-start(bf16[2,64,128]{2,1,0:T(8,128)(2,1)S(1)} %bitcast.592), channel_id=1, source_target_pairs={{8,0},{16,8},{24,16},{9,1},{17,9},{25,17},{10,2},{18,10},{26,18},{... | collective-permute-start | bytes 98312 | tf_op jit(solution)/shard_map/ppermute | solution.py:22
  180.0 4.7 %collective-permute-start.25 = (bf16[2,64,128]{2,1,0:T(8,128)(2,1)S(1)}, bf16[2,64,128]{2,1,0:T(8,128)(2,1)S(1)}, u32[]{:S(2)}, u32[]{:S(2)}) collective-permute-start(bf16[2,64,128]{2,1,0:T(8,128)(2,1)S(1)} %bitcast.600), channel_id=1, source_target_pairs={{0,8},{8,16},{16,24},{1,9},{9,17},{17,25},{2,10},{10,18},{18,26},{... | collective-permute-start | bytes 98312 | tf_op jit(solution)/shard_map/ppermute | solution.py:19
  183.1 5.8 %collective-permute-start.26 = (bf16[2,64,128]{2,1,0:T(8,128)(2,1)S(1)}, bf16[2,64,128]{2,1,0:T(8,128)(2,1)S(1)}, u32[]{:S(2)}, u32[]{:S(2)}) collective-permute-start(bf16[2,64,128]{2,1,0:T(8,128)(2,1)S(1)} %bitcast.593), channel_id=1, source_target_pairs={{8,0},{16,8},{24,16},{9,1},{17,9},{25,17},{10,2},{18,10},{26,18},{... | collective-permute-start | bytes 98312 | tf_op jit(solution)/shard_map/ppermute | solution.py:22
  190.2 4.9 %collective-permute-start.27 = (bf16[16,2,128]{2,1,0:T(2,128)(2,1)S(1)}, bf16[16,2,128]{2,1,0:T(2,128)(2,1)S(1)}, u32[]{:S(2)}, u32[]{:S(2)}) collective-permute-start(bf16[16,2,128]{2,1,0:T(2,128)(2,1)S(1)} %get-tuple-element.237), channel_id=1, source_target_pairs={{0,1},{1,2},{2,3},{3,4},{4,5},{5,6},{6,7},{7,0},{8,9},{9,10},{10,1... | collective-permute-start | bytes 24584 | tf_op jit(solution)/shard_map/ppermute | solution.py:19
  190.3 4.9 %collective-permute-start.28 = (bf16[16,2,128]{2,1,0:T(2,128)(2,1)S(1)}, bf16[16,2,128]{2,1,0:T(2,128)(2,1)S(1)}, u32[]{:S(2)}, u32[]{:S(2)}) collective-permute-start(bf16[16,2,128]{2,1,0:T(2,128)(2,1)S(1)} %get-tuple-element.236), channel_id=1, source_target_pairs={{1,0},{2,1},{3,2},{4,3},{5,4},{6,5},{7,6},{0,7},{9,8},{10,9},{11,1... | collective-permute-start | bytes 24584 | tf_op jit(solution)/shard_map/ppermute | solution.py:22
  197.1 4.9 %collective-permute-start.29 = (bf16[16,2,128]{2,1,0:T(2,128)(2,1)S(1)}, bf16[16,2,128]{2,1,0:T(2,128)(2,1)S(1)}, u32[]{:S(2)}, u32[]{:S(2)}) collective-permute-start(bf16[16,2,128]{2,1,0:T(2,128)(2,1)S(1)} %get-tuple-element.233), channel_id=1, source_target_pairs={{0,1},{1,2},{2,3},{3,4},{4,5},{5,6},{6,7},{7,0},{8,9},{9,10},{10,1... | collective-permute-start | bytes 24584 | tf_op jit(solution)/shard_map/ppermute | solution.py:19
  197.2 4.9 %collective-permute-start.30 = (bf16[16,2,128]{2,1,0:T(2,128)(2,1)S(1)}, bf16[16,2,128]{2,1,0:T(2,128)(2,1)S(1)}, u32[]{:S(2)}, u32[]{:S(2)}) collective-permute-start(bf16[16,2,128]{2,1,0:T(2,128)(2,1)S(1)} %get-tuple-element.232), channel_id=1, source_target_pairs={{1,0},{2,1},{3,2},{4,3},{5,4},{6,5},{7,6},{0,7},{9,8},{10,9},{11,1... | collective-permute-start | bytes 24584 | tf_op jit(solution)/shard_map/ppermute | solution.py:22
  203.6 4.4 %collective-permute-start.31 = (bf16[2,64,128]{2,1,0:T(8,128)(2,1)S(1)}, bf16[2,64,128]{2,1,0:T(8,128)(2,1)S(1)}, u32[]{:S(2)}, u32[]{:S(2)}) collective-permute-start(bf16[2,64,128]{2,1,0:T(8,128)(2,1)S(1)} %bitcast.601), channel_id=1, source_target_pairs={{0,8},{8,16},{16,24},{1,9},{9,17},{17,25},{2,10},{10,18},{18,26},{... | collective-permute-start | bytes 98312 | tf_op jit(solution)/shard_map/ppermute | solution.py:19
  206.5 5.8 %collective-permute-start.32 = (bf16[2,64,128]{2,1,0:T(8,128)(2,1)S(1)}, bf16[2,64,128]{2,1,0:T(8,128)(2,1)S(1)}, u32[]{:S(2)}, u32[]{:S(2)}) collective-permute-start(bf16[2,64,128]{2,1,0:T(8,128)(2,1)S(1)} %bitcast.594), channel_id=1, source_target_pairs={{8,0},{16,8},{24,16},{9,1},{17,9},{25,17},{10,2},{18,10},{26,18},{... | collective-permute-start | bytes 98312 | tf_op jit(solution)/shard_map/ppermute | solution.py:22
  213.9 4.7 %collective-permute-start.33 = (bf16[2,64,128]{2,1,0:T(8,128)(2,1)S(1)}, bf16[2,64,128]{2,1,0:T(8,128)(2,1)S(1)}, u32[]{:S(2)}, u32[]{:S(2)}) collective-permute-start(bf16[2,64,128]{2,1,0:T(8,128)(2,1)S(1)} %bitcast.602), channel_id=1, source_target_pairs={{0,8},{8,16},{16,24},{1,9},{9,17},{17,25},{2,10},{10,18},{18,26},{... | collective-permute-start | bytes 98312 | tf_op jit(solution)/shard_map/ppermute | solution.py:19
  217.0 5.8 %collective-permute-start.34 = (bf16[2,64,128]{2,1,0:T(8,128)(2,1)S(1)}, bf16[2,64,128]{2,1,0:T(8,128)(2,1)S(1)}, u32[]{:S(2)}, u32[]{:S(2)}) collective-permute-start(bf16[2,64,128]{2,1,0:T(8,128)(2,1)S(1)} %bitcast.595), channel_id=1, source_target_pairs={{8,0},{16,8},{24,16},{9,1},{17,9},{25,17},{10,2},{18,10},{26,18},{... | collective-permute-start | bytes 98312 | tf_op jit(solution)/shard_map/ppermute | solution.py:22
  224.2 4.9 %collective-permute-start.35 = (bf16[16,2,128]{2,1,0:T(2,128)(2,1)S(1)}, bf16[16,2,128]{2,1,0:T(2,128)(2,1)S(1)}, u32[]{:S(2)}, u32[]{:S(2)}) collective-permute-start(bf16[16,2,128]{2,1,0:T(2,128)(2,1)S(1)} %get-tuple-element.221), channel_id=1, source_target_pairs={{0,1},{1,2},{2,3},{3,4},{4,5},{5,6},{6,7},{7,0},{8,9},{9,10},{10,1... | collective-permute-start | bytes 24584 | tf_op jit(solution)/shard_map/ppermute | solution.py:19
  224.2 4.9 %collective-permute-start.36 = (bf16[16,2,128]{2,1,0:T(2,128)(2,1)S(1)}, bf16[16,2,128]{2,1,0:T(2,128)(2,1)S(1)}, u32[]{:S(2)}, u32[]{:S(2)}) collective-permute-start(bf16[16,2,128]{2,1,0:T(2,128)(2,1)S(1)} %get-tuple-element.220), channel_id=1, source_target_pairs={{1,0},{2,1},{3,2},{4,3},{5,4},{6,5},{7,6},{0,7},{9,8},{10,9},{11,1... | collective-permute-start | bytes 24584 | tf_op jit(solution)/shard_map/ppermute | solution.py:22
  231.1 4.9 %collective-permute-start.37 = (bf16[16,2,128]{2,1,0:T(2,128)(2,1)S(1)}, bf16[16,2,128]{2,1,0:T(2,128)(2,1)S(1)}, u32[]{:S(2)}, u32[]{:S(2)}) collective-permute-start(bf16[16,2,128]{2,1,0:T(2,128)(2,1)S(1)} %get-tuple-element.217), channel_id=1, source_target_pairs={{0,1},{1,2},{2,3},{3,4},{4,5},{5,6},{6,7},{7,0},{8,9},{9,10},{10,1... | collective-permute-start | bytes 24584 | tf_op jit(solution)/shard_map/ppermute | solution.py:19
  231.1 4.9 %collective-permute-start.38 = (bf16[16,2,128]{2,1,0:T(2,128)(2,1)S(1)}, bf16[16,2,128]{2,1,0:T(2,128)(2,1)S(1)}, u32[]{:S(2)}, u32[]{:S(2)}) collective-permute-start(bf16[16,2,128]{2,1,0:T(2,128)(2,1)S(1)} %get-tuple-element.216), channel_id=1, source_target_pairs={{1,0},{2,1},{3,2},{4,3},{5,4},{6,5},{7,6},{0,7},{9,8},{10,9},{11,1... | collective-permute-start | bytes 24584 | tf_op jit(solution)/shard_map/ppermute | solution.py:22
  237.6 4.4 %collective-permute-start.39 = (bf16[2,64,128]{2,1,0:T(8,128)(2,1)S(1)}, bf16[2,64,128]{2,1,0:T(8,128)(2,1)S(1)}, u32[]{:S(2)}, u32[]{:S(2)}) collective-permute-start(bf16[2,64,128]{2,1,0:T(8,128)(2,1)S(1)} %bitcast.603), channel_id=1, source_target_pairs={{0,8},{8,16},{16,24},{1,9},{9,17},{17,25},{2,10},{10,18},{18,26},{... | collective-permute-start | bytes 98312 | tf_op jit(solution)/shard_map/ppermute | solution.py:19
  240.4 5.8 %collective-permute-start.40 = (bf16[2,64,128]{2,1,0:T(8,128)(2,1)S(1)}, bf16[2,64,128]{2,1,0:T(8,128)(2,1)S(1)}, u32[]{:S(2)}, u32[]{:S(2)}) collective-permute-start(bf16[2,64,128]{2,1,0:T(8,128)(2,1)S(1)} %bitcast.596), channel_id=1, source_target_pairs={{8,0},{16,8},{24,16},{9,1},{17,9},{25,17},{10,2},{18,10},{26,18},{... | collective-permute-start | bytes 98312 | tf_op jit(solution)/shard_map/ppermute | solution.py:22
  247.9 4.7 %collective-permute-start.41 = (bf16[2,64,128]{2,1,0:T(8,128)(2,1)S(1)}, bf16[2,64,128]{2,1,0:T(8,128)(2,1)S(1)}, u32[]{:S(2)}, u32[]{:S(2)}) collective-permute-start(bf16[2,64,128]{2,1,0:T(8,128)(2,1)S(1)} %bitcast.604), channel_id=1, source_target_pairs={{0,8},{8,16},{16,24},{1,9},{9,17},{17,25},{2,10},{10,18},{18,26},{... | collective-permute-start | bytes 98312 | tf_op jit(solution)/shard_map/ppermute | solution.py:19
  251.0 5.8 %collective-permute-start.42 = (bf16[2,64,128]{2,1,0:T(8,128)(2,1)S(1)}, bf16[2,64,128]{2,1,0:T(8,128)(2,1)S(1)}, u32[]{:S(2)}, u32[]{:S(2)}) collective-permute-start(bf16[2,64,128]{2,1,0:T(8,128)(2,1)S(1)} %bitcast.597), channel_id=1, source_target_pairs={{8,0},{16,8},{24,16},{9,1},{17,9},{25,17},{10,2},{18,10},{26,18},{... | collective-permute-start | bytes 98312 | tf_op jit(solution)/shard_map/ppermute | solution.py:22
  (6 other events, 24.2 us)
where the time goes:
time: 259 us
  starting transfers between devices  91 us (35%)
  waiting for transfers between devices  62.5 us (24%)
  matrix products  40.9 us (16%)
  loops' own time  40.6 us (16%)
  local copies, waits for them, and re-layouts  17.4 us (7%)
  other arithmetic  5.05 us (2%)
    ppermute x18, starting transfers between devices, extended(): lax.ppermute(lax.slice_in_dim(block, 0, width, axis=dim), axis, backward)  44.7 us
    ppermute x18, waiting for transfers between devices, extended(): lax.ppermute(lax.slice_in_dim(block, 0, width, axis=dim), axis, backward)  41.3 us
    another operation x1, loops' own time, local(): lax.fori_loop(0, live, add_block, jnp.zeros((rows * cols, hid), jnp.float...  40.6 us
    ppermute x18, starting transfers between devices, extended(): lax.ppermute(lax.slice_in_dim(block, block.shape[dim] - width, None, axis...  36.2 us
    ppermute x18, waiting for transfers between devices, extended(): lax.ppermute(lax.slice_in_dim(block, block.shape[dim] - width, None, axis...  16.9 us
    dot_general x10, matrix products, add_block(): return total + jnp.dot(corr, proj, preferred_element_type=jnp.float32)  14.1 us
    dot_general x45, matrix products, conv_lon(): jnp.dot(piece, weight[tap], preferred_element_type=jnp.float32)  13.5 us
    dot_general x45, matrix products, conv_lat(): jnp.dot(piece, weight[tap], preferred_element_type=jnp.float32)  13.2 us
  transfers between devices with their start and end apart: 43, of which 29 were waited for; matrix products, arithmetic and copies ran while one was open for 2% of the time, Pallas kernels for 0%

commit v1 on v0

v1 whole, which is shorter than its diff:
```python
import functools

import jax
import jax.numpy as jnp
from jax import lax
from jax.experimental import pallas as pl
from jax.experimental.pallas import tpu as pltpu
from jax.sharding import PartitionSpec as P

POOLR = 8
POOLC = 16
RMAX = 4
ITERS = 4
HALO = 4
EDGE = 16
CTX, HID, MOT, STATE = 0, 1, 2, 3
MESH = pl.DeviceIdType.MESH
BF = jnp.bfloat16
F32 = jnp.float32


def sigmoid(value):
    return 0.5 * jnp.tanh(0.5 * value) + 0.5


def dot(left, right):
    return jnp.dot(left, right, preferred_element_type=F32)


def flat(value):
    return value.reshape(-1, value.shape[-1])


def kernel(
    n_lat,
    n_lon,
    offset_ref,
    class_ref,
    count_ref,
    one_ref,
    two_ref,
    ctx_ref,
    init_ref,
    proj_ref,
    input_ref,
    zr_ref,
    q_ref,
    ubias_ref,
    gbias_ref,
    out_ref,
    ext,
    side_l,
    side_r,
    pool,
    corr,
    projs,
    joined,
    xl_z,
    xl_r,
    xl_q,
    xt_z,
    xt_r,
    xt_q,
    s_lon,
    s_lat,
    rs_lon,
    rs_lat,
    z_lon,
    z_lat,
    send_sem,
    recv_sem,
    pool_send,
    pool_recv,
    pass_send,
):
    rows, cols, chans = one_ref.shape
    hid = init_ref.shape[2]
    wide = cols + 16
    near = cols + 8
    slots = offset_ref.shape[2]
    lat, lon = lax.axis_index("lat"), lax.axis_index("lon")
    north, south = lax.rem(lat + n_lat - 1, n_lat), lax.rem(lat + 1, n_lat)
    west, east = lax.rem(lon + n_lon - 1, n_lon), lax.rem(lon + 1, n_lon)
    has_n, has_s = lat > 0, lat < n_lat - 1
    parity = lax.rem(lon, 2)
    lowest = -min(RMAX, (n_lon - 1) // 2)
    highest = min(RMAX, n_lon // 2)

    def place(offset):
        return lax.rem(offset - lowest + n_lon, n_lon)

    def along(steps):
        return lax.rem(lon + steps + n_lon, n_lon)

    evens = [d for d in (2, -2, 4, -4) if lowest <= d <= highest]

    barrier = pltpu.get_barrier_semaphore()
    partners = [1, -1] + evens
    for steps in partners:
        pl.semaphore_signal(
            barrier, inc=1, device_id=(lat, along(steps)), device_id_type=MESH
        )

    @pl.when(has_n)
    def _():
        for column in (west, lon, east):
            pl.semaphore_signal(barrier, inc=1, device_id=(north, column), device_id_type=MESH)

    @pl.when(has_s)
    def _():
        for column in (west, lon, east):
            pl.semaphore_signal(barrier, inc=1, device_id=(south, column), device_id_type=MESH)

    top = slice(HALO, 2 * HALO)
    bottom = slice(rows, rows + HALO)
    above = slice(0, HALO)
    below = slice(rows + HALO, rows + 2 * HALO)
    body = slice(HALO, HALO + rows)
    first, last = slice(0, EDGE), slice(cols - EDGE, cols)
    panel = slice(0, cols)

    def copy(e, way):
        src, dst, device = (
            lambda: (ext.at[e, top, panel], ext.at[e, below, panel], (north, lon)),
            lambda: (ext.at[e, bottom, panel], ext.at[e, above, panel], (south, lon)),
            lambda: (ext.at[e, body, last], side_l.at[e, body], (lat, east)),
            lambda: (ext.at[e, body, first], side_r.at[e, body], (lat, west)),
            lambda: (ext.at[e, top, last], side_l.at[e, below], (north, east)),
            lambda: (ext.at[e, top, first], side_r.at[e, below], (north, west)),
            lambda: (ext.at[e, bottom, last], side_l.at[e, above], (south, east)),
            lambda: (ext.at[e, bottom, first], side_r.at[e, above], (south, west)),
        )[way]()
        return pltpu.make_async_remote_copy(
            src_ref=src,
            dst_ref=dst,
            send_sem=send_sem.at[e, way],
            recv_sem=recv_sem.at[e, way],
            device_id=device,
            device_id_type=MESH,
        )

    to_north, to_south, to_side = (0, 4, 5), (1, 6, 7), (2, 3)

    def send(e, full=True):
        if full:

            @pl.when(has_n)
            def _():
                for way in to_north:
                    copy(e, way).start()

            @pl.when(has_s)
            def _():
                for way in to_south:
                    copy(e, way).start()

        for way in to_side:
            copy(e, way).start()

    def receive(e, full=True):
        if full:

            @pl.when(has_s)
            def _():
                for way in to_north:
                    copy(e, way).wait_recv()
                for way in to_south:
                    copy(e, way).wait_send()

            @pl.when(jnp.logical_not(has_s))
            def _():
                ext[e, below] = jnp.zeros((HALO, wide, hid), BF)
                side_l[e, below] = jnp.zeros((HALO, EDGE, hid), BF)
                side_r[e, below] = jnp.zeros((HALO, EDGE, hid), BF)

            @pl.when(has_n)
            def _():
                for way in to_south:
                    copy(e, way).wait_recv()
                for way in to_north:
                    copy(e, way).wait_send()

            @pl.when(jnp.logical_not(has_n))
            def _():
                ext[e, above] = jnp.zeros((HALO, wide, hid), BF)
                side_l[e, above] = jnp.zeros((HALO, EDGE, hid), BF)
                side_r[e, above] = jnp.zeros((HALO, EDGE, hid), BF)

        for way in to_side:
            copy(e, way).wait()
        part = slice(None) if full else body
        right = side_r[e, part].astype(F32)
        left = side_l[e, part].astype(F32)
        spot = lax.broadcasted_iota(jnp.int32, right.shape, 1)
        merged = jnp.where(spot < 8, right, left)
        ext[e, part, cols:] = merged.astype(BF)

    def spread(e, target):
        target[:, 8 : 8 + cols] = ext[e, body, panel].astype(F32)
        sides = ext[e, body, cols:].astype(F32)
        target[:, 8 + cols :] = sides[:, 0:8]
        target[:, 0:8] = sides[:, 8:16]

    point = lax.broadcasted_iota(jnp.int32, (POOLC, 2 * cols), 0)
    cell = lax.rem(lax.broadcasted_iota(jnp.int32, (POOLC, 2 * cols), 1), cols)
    pool_rows, pool_cols = rows // POOLR, cols // POOLC
    inside = (cell >= point * pool_cols) & (cell < (point + 1) * pool_cols)
    window = jnp.where(inside, 1.0 / (pool_rows * pool_cols), 0.0).astype(BF)
    for index in range(POOLR):
        block = flat(two_ref[pool_rows * index : pool_rows * (index + 1)])
        pool[-lowest, POOLC * index : POOLC * (index + 1)] = dot(window, block).astype(BF)
    ext[CTX, body, panel] = ctx_ref[...]
    ext[HID, body, panel] = init_ref[...]

    lat_partners = 3 * has_n.astype(jnp.int32) + 3 * has_s.astype(jnp.int32)
    pl.semaphore_wait(barrier, len(partners) + lat_partners)

    def direct(steps):
        return pltpu.make_async_remote_copy(
            src_ref=pool.at[-lowest],
            dst_ref=pool.at[place(-steps)],
            send_sem=pool_send.at[evens.index(steps)],
            recv_sem=pool_recv.at[place(-steps)],
            device_id=(lat, along(steps)),
            device_id_type=MESH,
        )

    sibling = lon + 1 - 2 * parity

    def forward(number, source):
        target = source - 1 + 2 * parity
        return pltpu.make_async_remote_copy(
            src_ref=pool.at[place(source)],
            dst_ref=pool.at[place(target)],
            send_sem=pass_send.at[number],
            recv_sem=pool_recv.at[place(target)],
            device_id=(lat, sibling),
            device_id_type=MESH,
        )

    def arrived(spot):
        return pltpu.make_async_remote_copy(
            src_ref=pool.at[-lowest],
            dst_ref=pool.at[spot],
            send_sem=pool_send.at[0],
            recv_sem=pool_recv.at[spot],
            device_id=(lat, sibling),
            device_id_type=MESH,
        ).wait_recv()

    send(CTX)
    for steps in evens:
        direct(steps).start()
    forward(0, 0).start()
    send(HID, False)

    def inputs_lon(part, base):
        weight = [
            input_ref[0, tap, part * hid : (part + 1) * hid, :] for tap in range(5)
        ]
        weight = jnp.concatenate(weight, axis=0)
        step = rows // 2

        def chunk(index, carry):
            at = pl.ds(index * step, step)
            pieces = [flat(joined[at, 2 + k : 2 + k + near]).astype(BF) for k in range(5)]
            total = dot(jnp.concatenate(pieces, axis=1), weight)
            for place_, store in enumerate((xl_z, xl_r, xl_q)):
                value = total[:, place_ * hid : (place_ + 1) * hid].reshape(step, near, hid)
                if base is None:
                    store[at] = store[at] + value
                else:
                    store[at] = value + base[place_]
            return carry

        lax.fori_loop(0, 2, chunk, 0)

    def inputs_lat(part, e, base):
        weight = [
            input_ref[1, tap, part * hid : (part + 1) * hid, :] for tap in range(5)
        ]
        weight = jnp.concatenate(weight, axis=0)
        step = (rows + 4) // 2

        def chunk(index, carry):
            start = index * step
            at = pl.ds(start, step)
            pieces = [flat(ext[e, pl.ds(start + k, step)]) for k in range(5)]
            total = dot(jnp.concatenate(pieces, axis=1), weight)
            for place_, store in enumerate((xt_z, xt_r, xt_q)):
                value = total[:, place_ * hid : (place_ + 1) * hid].reshape(step, wide, hid)
                if base is None:
                    store[at] = store[at] + value
                else:
                    store[at] = value + base[place_]
            return carry

        lax.fori_loop(0, 2, chunk, 0)

    def biases(index):
        gate = gbias_ref[index : index + 1]
        parts = ubias_ref[index : index + 1], gate[:, :hid], gate[:, hid:]
        return [part.reshape(1, 1, hid) for part in parts]

    receive(CTX)
    spread(CTX, joined)
    inputs_lon(0, biases(0))
    inputs_lat(0, CTX, biases(1))

    scale = chans ** (-0.5)

    def correlate(spot):
        keys = pool[spot]
        step = rows // 4

        def chunk(index, carry):
            queries = flat(one_ref[pl.ds(index * step, step)])
            value = lax.dot_general(
                queries, keys, (((1,), (1,)), ((), ())), preferred_element_type=F32
            )
            corr[spot, pl.ds(index * step, step)] = (
                (value * scale).astype(BF).reshape(step, cols, -1)
            )
            return carry

        lax.fori_loop(0, 4, chunk, 0)

    correlate(-lowest)
    sources = [-2, 2, 4 - 8 * parity]
    for number, source in enumerate(sources):
        arrived(place(source))
        forward(number + 1, source).start()
    if n_lon > 2 * RMAX:
        arrived(place(4 * (2 * parity - 1)))
    for steps in evens:
        correlate(place(steps))
    for steps in (-1, 1, -3, 3):
        arrived(place(steps))
        correlate(place(steps))
    for steps in evens:
        direct(steps).wait_send()
    for number, source in enumerate([0] + sources):
        forward(number, source).wait_send()

    live = count_ref[0, 0]
    spots = []
    for slot in range(slots):
        offset = offset_ref[0, 0, slot]
        spots.append(jnp.where(offset < lowest, offset + n_lon, offset) - lowest)
        weight = proj_ref[class_ref[0, 0, slot]].astype(F32)
        weight = jnp.where(slot < live, weight, 0.0)
        projs[slot * weight.shape[0] : (slot + 1) * weight.shape[0]] = weight.astype(BF)

    quarter = rows // 4

    def move(index, carry):
        at = pl.ds(index * quarter, quarter)
        pieces = [flat(corr[spot, at]) for spot in spots]
        total = dot(jnp.concatenate(pieces, axis=1), projs[...])
        moved = jnp.maximum(total, 0.0).astype(BF).reshape(quarter, cols, hid)
        ext[MOT, pl.ds(HALO + index * quarter, quarter), panel] = moved
        return carry

    lax.fori_loop(0, 4, move, 0)
    send(MOT)
    receive(HID, False)
    spread(HID, s_lon)
    receive(MOT)
    spread(MOT, joined)
    inputs_lon(1, None)
    inputs_lat(1, MOT, None)

    def pass_lon(e):
        step = rows // 2

        def gates(index, carry):
            at = pl.ds(index * step, step)
            pieces = [flat(s_lon[at, 2 + k : 2 + k + near]).astype(BF) for k in range(5)]
            mixed = dot(jnp.concatenate(pieces, axis=1), zr_ref[0])
            z_lon[at] = sigmoid(xl_z[at] + mixed[:, :hid].reshape(step, near, hid))
            reset = sigmoid(xl_r[at] + mixed[:, hid:].reshape(step, near, hid))
            rs_lon[at] = reset * s_lon[at, 4 : 4 + near]
            return carry

        lax.fori_loop(0, 2, gates, 0)

        def update(index, carry):
            at = pl.ds(index * step, step)
            pieces = [flat(rs_lon[at, 2 + k : 2 + k + cols]).astype(BF) for k in range(5)]
            mixed = dot(jnp.concatenate(pieces, axis=1), q_ref[0]).reshape(step, cols, hid)
            candidate = jnp.tanh(xl_q[at, 4 : 4 + cols] + mixed)
            state = s_lon[at, 8 : 8 + cols]
            z = z_lon[at, 4 : 4 + cols]
            state = (1.0 - z) * state + z * candidate
            inner = pl.ds(HALO + index * step, step)
            s_lat[inner, panel] = state
            ext[e, inner, panel] = state.astype(BF)
            return carry

        lax.fori_loop(0, 2, update, 0)

    def pass_lat(e):
        s_lat[above] = ext[e, above].astype(F32)
        s_lat[below] = ext[e, below].astype(F32)
        s_lat[body, cols:] = ext[e, body, cols:].astype(F32)
        step = (rows + 4) // 2

        def gates(index, carry):
            start = index * step
            at = pl.ds(start, step)
            pieces = [flat(ext[e, pl.ds(start + k, step)]) for k in range(5)]
            mixed = dot(jnp.concatenate(pieces, axis=1), zr_ref[1])
            z_lat[at] = sigmoid(xt_z[at] + mixed[:, :hid].reshape(step, wide, hid))
            reset = sigmoid(xt_r[at] + mixed[:, hid:].reshape(step, wide, hid))
            rs_lat[at] = (reset * s_lat[pl.ds(start + 2, step)]).astype(BF)
            return carry

        lax.fori_loop(0, 2, gates, 0)
        half = rows // 2

        def update(index, carry):
            start = index * half
            at = pl.ds(start, half)
            pieces = [flat(rs_lat[pl.ds(start + k, half)]) for k in range(5)]
            mixed = dot(jnp.concatenate(pieces, axis=1), q_ref[1]).reshape(half, wide, hid)
            candidate = jnp.tanh(xt_q[pl.ds(start + 2, half)] + mixed)
            state = s_lat[pl.ds(start + HALO, half)]
            z = z_lat[pl.ds(start + 2, half)]
            state = (1.0 - z) * state + z * candidate
            s_lon[at, 8 : 8 + cols] = state[:, panel]
            s_lon[at, 8 + cols :] = state[:, cols : cols + 8]
            s_lon[at, 0:8] = state[:, cols + 8 :]
            return carry

        lax.fori_loop(0, 2, update, 0)

    def iteration(index, carry):
        e = STATE + index
        pass_lon(e)
        send(e)
        receive(e)
        pass_lat(e)
        return carry

    lax.fori_loop(0, ITERS, iteration, 0)
    out_ref[...] = s_lon[:, 8 : 8 + cols].astype(BF)


def local(
    n_lat,
    n_lon,
    feat_one,
    feat_two,
    context_in,
    hidden_init,
    corr_proj,
    input_conv,
    state_zr,
    state_q,
    update_bias,
    gate_bias,
    blk_offset,
    blk_class,
    blk_count,
):
    rows, cols, chans = feat_one.shape
    hid = hidden_init.shape[2]
    points = POOLR * POOLC
    slots = blk_offset.shape[2]
    reach = min(n_lon, 2 * RMAX + 1)
    wide, near = cols + 16, cols + 8
    tall = rows + 2 * HALO
    count = STATE + ITERS
    taps = state_zr.shape[1]
    state_zr = state_zr.reshape(2, taps * hid, 2 * hid)
    state_q = state_q.reshape(2, taps * hid, hid)
    vmem = pl.BlockSpec(memory_space=pltpu.VMEM)
    smem = pl.BlockSpec(memory_space=pltpu.SMEM)
    return pl.pallas_call(
        functools.partial(kernel, n_lat, n_lon),
        out_shape=jax.ShapeDtypeStruct((rows, cols, hid), BF),
        in_specs=[smem] * 3 + [vmem] * 10,
        out_specs=vmem,
        scratch_shapes=[
            pltpu.VMEM((count, tall, wide, hid), BF),
            pltpu.VMEM((count, tall, EDGE, hid), BF),
            pltpu.VMEM((count, tall, EDGE, hid), BF),
            pltpu.VMEM((reach, points, chans), BF),
            pltpu.VMEM((reach, rows, cols, points), BF),
            pltpu.VMEM((slots * points, hid), BF),
            pltpu.VMEM((rows, wide, hid), F32),
            pltpu.VMEM((rows, near, hid), F32),
            pltpu.VMEM((rows, near, hid), F32),
            pltpu.VMEM((rows, near, hid), F32),
            pltpu.VMEM((rows + 4, wide, hid), F32),
            pltpu.VMEM((rows + 4, wide, hid), F32),
            pltpu.VMEM((rows + 4, wide, hid), F32),
            pltpu.VMEM((rows, wide, hid), F32),
            pltpu.VMEM((tall, wide, hid), F32),
            pltpu.VMEM((rows, near, hid), F32),
            pltpu.VMEM((rows + 4, wide, hid), BF),
            pltpu.VMEM((rows, near, hid), F32),
            pltpu.VMEM((rows + 4, wide, hid), F32),
            pltpu.SemaphoreType.DMA((count, 8)),
            pltpu.SemaphoreType.DMA((count, 8)),
            pltpu.SemaphoreType.DMA((4,)),
            pltpu.SemaphoreType.DMA((reach,)),
            pltpu.SemaphoreType.DMA((4,)),
        ],
        compiler_params=pltpu.CompilerParams(
            collective_id=0, has_side_effects=True, vmem_limit_bytes=52 * 1024 * 1024
        ),
        name="refine",
    )(
        blk_offset,
        blk_class,
        blk_count,
        feat_one,
        feat_two,
        context_in,
        hidden_init,
        corr_proj,
        input_conv,
        state_zr,
        state_q,
        update_bias,
        gate_bias,
    )


def solution(mesh):
    placed = (
        P("lat", "lon", None),
        P("lat", "lon", None),
        P("lat", "lon", None),
        P("lat", "lon", None),
        P(),
        P(),
        P(),
        P(),
        P(),
        P(),
        P("lat", "lon", None),
        P("lat", "lon", None),
        P("lat", "lon"),
    )
    return jax.shard_map(
        functools.partial(local, mesh.shape["lat"], mesh.shape["lon"]),
        mesh=mesh,
        in_specs=placed,
        out_specs=P("lat", "lon", None),
        check_vma=False,
    )
```

time: 259 us -> 78.6 us (0.30)
  starting transfers between devices: 91 us -> 0 us
  Pallas kernels: 0 us -> 68.9 us
  waiting for transfers between devices: 62.5 us -> 0 us
  matrix products: 40.9 us -> 0 us
  loops' own time: 40.6 us -> 0 us
  local copies, waits for them, and re-layouts: 17.4 us -> 8.23 us
  other arithmetic: 5.05 us -> 0 us
    ppermute x43 -> x0, starting transfers between devices: 91 us -> none  [the longest x18 44.7 us: extended(): lax.ppermute(lax.slice_in_dim(block, 0, width, axis=dim), axis, backward)]
    pallas_call x0 -> x1, Pallas kernels: none -> 68.9 us  [local(): pl.pallas_call(functools.partial(kernel, n_lat, n_lon), out_shape=jax.Sha...]
    ppermute x43 -> x0, waiting for transfers between devices: 62.5 us -> none  [the longest x18 41.3 us: extended(): lax.ppermute(lax.slice_in_dim(block, 0, width, axis=dim), axis, backward)]
    dot_general x100 -> x0, matrix products: 40.9 us -> none  [the longest x10 14.1 us: add_block(): return total + jnp.dot(corr, proj, preferred_element_type=jnp.float32)]
    another operation x1 -> x0, loops' own time: 40.6 us -> none  [local(): lax.fori_loop(0, live, add_block, jnp.zeros((rows * cols, hid), jnp.float...]
    dynamic_slice x20 -> x0, local copies, waits for them, and re-layouts: 13.1 us -> none  [the longest x10 6.56 us: add_block(): keys = pick(offsets[slot])]
    unnamed x30 -> x19, local copies, waits for them, and re-layouts: 1.69 us -> 8.23 us
    concatenate x18 -> x0, other arithmetic: 3.27 us -> none  [extended(): block = jnp.concatenate([low, block, high], axis=dim)]
  transfers between devices with their start and end apart: 43 -> 0, of which waited for: 29 -> 0; matrix products, arithmetic and copies ran while one was open for 2% -> 0% of each run, Pallas kernels for 0% -> 0%
where the time goes in v1:
time: 78.6 us; the launch traced here: 77.8 us
  Pallas kernels  68.9 us (88%)
  local copies, waits for them, and re-layouts  8.23 us (10%)
    pallas_call x1, Pallas kernels, local(): pl.pallas_call(functools.partial(kernel, n_lat, n_lon), out_shape=jax.Sha...  68.9 us
    unnamed x19, local copies, waits for them, and re-layouts  8.23 us

profile of v1, /device:TPU:0, one launch (start us, length us, event | category | flops | bytes accessed | tf_op | source)
XLA Modules:
  0.0 77.8 jit_solution(13580259017445519920)
XLA Ops:
  0.7 0.0 copy-start
  0.7 1.0 %copy-done = bf16[16,64,256]{2,1,0:T(8,128)(2,1)S(1)} copy-done((bf16[16,64,256]{2,1,0:T(8,128)(2,1)S(1)}, bf16[16,64,256]{2,1,0:T(8,128)(2,1)}, u32[]{:S(2)}) %copy-start) | copy-done | bytes 524312
  1.7 0.0 copy-start.1
  1.7 1.0 %copy-done.1 = bf16[2,5,128,128]{3,2,1,0:T(8,128)(2,1)S(1)} copy-done((bf16[2,5,128,128]{3,2,1,0:T(8,128)(2,1)S(1)}, bf16[2,5,128,128]{3,2,1,0:T(8,128)(2,1)}, u32[]{:S(2)}) %copy-start.1) | copy-done | bytes 327704
  2.7 0.0 copy-start.2
  2.7 0.9 %copy-done.2 = bf16[16,64,128]{2,1,0:T(8,128)(2,1)S(1)} copy-done((bf16[16,64,128]{2,1,0:T(8,128)(2,1)S(1)}, bf16[16,64,128]{2,1,0:T(8,128)(2,1)}, u32[]{:S(2)}) %copy-start.2) | copy-done | bytes 262168
  3.6 0.0 copy-start.3
  3.6 0.9 %copy-done.3 = bf16[16,64,128]{2,1,0:T(8,128)(2,1)S(1)} copy-done((bf16[16,64,128]{2,1,0:T(8,128)(2,1)S(1)}, bf16[16,64,128]{2,1,0:T(8,128)(2,1)}, u32[]{:S(2)}) %copy-start.3) | copy-done | bytes 262168
  4.6 0.0 copy-start.4
  4.6 0.9 %copy-done.4 = bf16[8,128,128]{2,1,0:T(8,128)(2,1)S(1)} copy-done((bf16[8,128,128]{2,1,0:T(8,128)(2,1)S(1)}, bf16[8,128,128]{2,1,0:T(8,128)(2,1)}, u32[]{:S(2)}) %copy-start.4) | copy-done | bytes 262168
  5.5 0.0 copy-start.5
  5.5 0.7 copy-done.5
  6.2 0.0 copy-start.6
  6.2 0.7 copy-done.6
  6.9 0.0 copy-start.7
  6.9 0.7 copy-done.7
  7.5 0.0 copy-start.8
  7.5 0.7 copy-done.8
  8.2 68.9 %refine.1 = bf16[16,64,128]{2,1,0:T(8,128)(2,1)S(1)} custom-call(s32[1,1,12]{2,1,0:T(1,128)S(1)} %copy-done.7, s32[1,1,12]{2,1,0:T(1,128)S(1)} %copy-done.8, s32[1,1]{1,0:T(1,128)S(6)} %copy.15.count_ref, bf16[16,64,256]{2,1,0:T(8,128)(2,1)S(1)} %copy-done, bf16[16,64,256]{2,1,0:T(8,128)(2,1)} %two_ref.1, bf16[16,64,128]{2,1,0:T(8,128)(2,1)S(1)} %copy-done.2, ...), custom_call_target="tpu_custom_call" | custom-call | tf_op jit(solution)/shard_map/refine/pallas_call | solution.py:479
  77.1 0.7 copy.16
Async XLA Ops:
  0.7 1.0 %copy-start = (bf16[16,64,256]{2,1,0:T(8,128)(2,1)S(1)}, bf16[16,64,256]{2,1,0:T(8,128)(2,1)}, u32[]{:S(2)}) copy-start(bf16[16,64,256]{2,1,0:T(8,128)(2,1)} %one_ref.1) | copy-start | bytes 1572868
  1.7 1.0 %copy-start.1 = (bf16[2,5,128,128]{3,2,1,0:T(8,128)(2,1)S(1)}, bf16[2,5,128,128]{3,2,1,0:T(8,128)(2,1)}, u32[]{:S(2)}) copy-start(bf16[2,5,128,128]{3,2,1,0:T(8,128)(2,1)} %param.20) | copy-start | bytes 983044
  2.7 0.9 %copy-start.2 = (bf16[16,64,128]{2,1,0:T(8,128)(2,1)S(1)}, bf16[16,64,128]{2,1,0:T(8,128)(2,1)}, u32[]{:S(2)}) copy-start(bf16[16,64,128]{2,1,0:T(8,128)(2,1)} %ctx_ref.1) | copy-start | bytes 786436
  3.6 0.9 %copy-start.3 = (bf16[16,64,128]{2,1,0:T(8,128)(2,1)S(1)}, bf16[16,64,128]{2,1,0:T(8,128)(2,1)}, u32[]{:S(2)}) copy-start(bf16[16,64,128]{2,1,0:T(8,128)(2,1)} %init_ref.1) | copy-start | bytes 786436
  4.6 0.9 %copy-start.4 = (bf16[8,128,128]{2,1,0:T(8,128)(2,1)S(1)}, bf16[8,128,128]{2,1,0:T(8,128)(2,1)}, u32[]{:S(2)}) copy-start(bf16[8,128,128]{2,1,0:T(8,128)(2,1)} %proj_ref.1) | copy-start | bytes 786436
  5.5 0.7 copy-start.5
  6.2 0.7 copy-start.6
  6.9 0.7 copy-start.7
  7.5 0.7 copy-start.8

commit v2 on v1

v2 whole, which is shorter than its diff:
```python
import functools

import jax
import jax.numpy as jnp
from jax import lax
from jax.experimental import pallas as pl
from jax.experimental.pallas import tpu as pltpu
from jax.sharding import PartitionSpec as P

POOLR = 8
POOLC = 16
RMAX = 4
ITERS = 4
HALO = 4
CTX, MOT, STATE = 0, 1, 2
MESH = pl.DeviceIdType.MESH
BF = jnp.bfloat16
F32 = jnp.float32


def sigmoid(value):
    return 0.5 * jnp.tanh(0.5 * value) + 0.5


def dot(left, right):
    return jnp.dot(left, right, preferred_element_type=F32)


def flat(value):
    return value.reshape(-1, value.shape[-1])


def joined_up(parts, axis):
    return parts[0] if len(parts) == 1 else jnp.concatenate(parts, axis=axis)


def kernel(
    n_lat,
    n_lon,
    offset_ref,
    class_ref,
    count_ref,
    one_hbm,
    two_hbm,
    ctx_hbm,
    init_hbm,
    proj_hbm,
    input_hbm,
    zr_hbm,
    q_hbm,
    ubias_ref,
    gbias_ref,
    out_ref,
    one_ref,
    two_ref,
    init_ref,
    proj_ref,
    input_ref,
    zr_ref,
    q_ref,
    ext,
    side_out,
    side_in,
    pool,
    corr,
    projs,
    joined,
    xl_z,
    xl_r,
    xl_q,
    xt_z,
    xt_r,
    xt_q,
    s_lon,
    s_lat,
    rs_lon,
    rs_lat,
    z_lon,
    z_lat,
    load_sem,
    ns_send,
    ns_recv,
    ew_send,
    ew_recv,
    pool_send,
    pool_recv,
    pass_send,
):
    rows, cols, chans = one_ref.shape
    hid = init_ref.shape[2]
    near = cols + 8
    slots = offset_ref.shape[2]
    lat, lon = lax.axis_index("lat"), lax.axis_index("lon")
    north, south = lax.rem(lat + n_lat - 1, n_lat), lax.rem(lat + 1, n_lat)
    west, east = lax.rem(lon + n_lon - 1, n_lon), lax.rem(lon + 1, n_lon)
    has_n, has_s = lat > 0, lat < n_lat - 1
    parity = lax.rem(lon, 2)
    lowest = -min(RMAX, (n_lon - 1) // 2)
    highest = min(RMAX, n_lon // 2)

    top = slice(HALO, 2 * HALO)
    bottom = slice(rows, rows + HALO)
    above = slice(0, HALO)
    below = slice(rows + HALO, rows + 2 * HALO)
    body = slice(HALO, HALO + rows)
    main = slice(8, 8 + cols)

    loads = [
        pltpu.make_async_copy(source, target, load_sem.at[number])
        for number, (source, target) in enumerate(
            (
                (two_hbm, two_ref),
                (ctx_hbm, ext.at[CTX, body]),
                (init_hbm, init_ref),
                (input_hbm, input_ref),
                (one_hbm, one_ref),
                (proj_hbm, proj_ref),
                (zr_hbm, zr_ref),
                (q_hbm, q_ref),
            )
        )
    ]
    for load in loads:
        load.start()

    def place(offset):
        return lax.rem(offset - lowest + n_lon, n_lon)

    def along(steps):
        return lax.rem(lon + steps + n_lon, n_lon)

    evens = [d for d in (2, -2, 4, -4) if lowest <= d <= highest]

    barrier = pltpu.get_barrier_semaphore()
    partners = [1, -1] + evens
    for steps in partners:
        pl.semaphore_signal(
            barrier, inc=1, device_id=(lat, along(steps)), device_id_type=MESH
        )

    @pl.when(has_n)
    def _():
        pl.semaphore_signal(barrier, inc=1, device_id=(north, lon), device_id_type=MESH)

    @pl.when(has_s)
    def _():
        pl.semaphore_signal(barrier, inc=1, device_id=(south, lon), device_id_type=MESH)

    def to_lat(e, way):
        return pltpu.make_async_remote_copy(
            src_ref=ext.at[e, bottom if way else top],
            dst_ref=ext.at[e, above if way else below],
            send_sem=ns_send.at[e, way],
            recv_sem=ns_recv.at[e, way],
            device_id=(south if way else north, lon),
            device_id_type=MESH,
        )

    def to_lon(e, way):
        return pltpu.make_async_remote_copy(
            src_ref=side_out.at[e, way],
            dst_ref=side_in.at[e, 1 - way],
            send_sem=ew_send.at[e, way],
            recv_sem=ew_recv.at[e, way],
            device_id=(lat, east if way else west),
            device_id_type=MESH,
        )

    def send_lat(e):
        @pl.when(has_n)
        def _():
            to_lat(e, 0).start()

        @pl.when(has_s)
        def _():
            to_lat(e, 1).start()

    def receive_lat(e):
        @pl.when(has_s)
        def _():
            to_lat(e, 0).wait_recv()
            to_lat(e, 1).wait_send()

        @pl.when(jnp.logical_not(has_s))
        def _():
            ext[e, below] = jnp.zeros((HALO, cols, hid), BF)

        @pl.when(has_n)
        def _():
            to_lat(e, 1).wait_recv()
            to_lat(e, 0).wait_send()

        @pl.when(jnp.logical_not(has_n))
        def _():
            ext[e, above] = jnp.zeros((HALO, cols, hid), BF)

    def send_lon(e, low, high):
        for way, value in enumerate((low, high)):
            side_out[e, way] = value.reshape(rows // 2, 16, hid).astype(BF)
        for way in range(2):
            to_lon(e, way).start()

    def receive_lon(e, target):
        for way in range(2):
            to_lon(e, way).wait()
        target[:, 0:8] = side_in[e, 0].astype(F32).reshape(rows, 8, hid)
        target[:, 8 + cols :] = side_in[e, 1].astype(F32).reshape(rows, 8, hid)

    def direct(steps):
        return pltpu.make_async_remote_copy(
            src_ref=pool.at[-lowest],
            dst_ref=pool.at[place(-steps)],
            send_sem=pool_send.at[evens.index(steps)],
            recv_sem=pool_recv.at[place(-steps)],
            device_id=(lat, along(steps)),
            device_id_type=MESH,
        )

    sibling = lon + 1 - 2 * parity

    def forward(number, source):
        target = source - 1 + 2 * parity
        return pltpu.make_async_remote_copy(
            src_ref=pool.at[place(source)],
            dst_ref=pool.at[place(target)],
            send_sem=pass_send.at[number],
            recv_sem=pool_recv.at[place(target)],
            device_id=(lat, sibling),
            device_id_type=MESH,
        )

    def arrived(spot):
        return pltpu.make_async_remote_copy(
            src_ref=pool.at[-lowest],
            dst_ref=pool.at[spot],
            send_sem=pool_send.at[0],
            recv_sem=pool_recv.at[spot],
            device_id=(lat, sibling),
            device_id_type=MESH,
        ).wait_recv()

    point = lax.broadcasted_iota(jnp.int32, (POOLC, 2 * cols), 0)
    cell = lax.rem(lax.broadcasted_iota(jnp.int32, (POOLC, 2 * cols), 1), cols)
    pool_rows, pool_cols = rows // POOLR, cols // POOLC
    inside = (cell >= point * pool_cols) & (cell < (point + 1) * pool_cols)
    window = jnp.where(inside, 1.0 / (pool_rows * pool_cols), 0.0).astype(BF)
    loads[0].wait()
    for index in range(POOLR):
        block = flat(two_ref[pool_rows * index : pool_rows * (index + 1)])
        pool[-lowest, POOLC * index : POOLC * (index + 1)] = dot(window, block).astype(BF)

    lat_partners = has_n.astype(jnp.int32) + has_s.astype(jnp.int32)
    pl.semaphore_wait(barrier, len(partners) + lat_partners)
    for steps in evens:
        direct(steps).start()
    forward(0, 0).start()
    loads[1].wait()
    send_lat(CTX)
    whole = ext[CTX, body].astype(F32)
    joined[:, main] = whole
    send_lon(CTX, whole[:, 0:8], whole[:, cols - 8 :])
    loads[2].wait()
    whole = init_ref[...].astype(F32)
    s_lon[:, main] = whole
    send_lon(STATE, whole[:, 0:8], whole[:, cols - 8 :])

    def weights(index, part):
        channels = slice(part * hid, (part + 1) * hid)
        return jnp.concatenate([input_ref[index, tap, channels, :] for tap in range(5)], axis=0)

    def biases(index):
        gate = gbias_ref[index : index + 1]
        parts = ubias_ref[index : index + 1], gate[:, :hid], gate[:, hid:]
        return [part.reshape(1, 1, hid) for part in parts]

    def keep(stores, at, total, shape, base):
        for number, store in enumerate(stores):
            value = total[:, number * hid : (number + 1) * hid].reshape(shape)
            store[at] = value + (store[at] if base is None else base[number])

    def inputs_lon(part, base):
        weight = weights(0, part)
        step = rows // 2

        def chunk(index, carry):
            at = pl.ds(index * step, step)
            pieces = [flat(joined[at, 2 + k : 2 + k + near]).astype(BF) for k in range(5)]
            total = dot(jnp.concatenate(pieces, axis=1), weight)
            keep((xl_z, xl_r, xl_q), at, total, (step, near, hid), base)
            return carry

        lax.fori_loop(0, 2, chunk, 0)

    def inputs_lat(part, e, base, blocks):
        weight = weights(1, part)
        for start, size in blocks:
            pieces = [flat(ext[e, start + k : start + k + size]) for k in range(5)]
            total = dot(jnp.concatenate(pieces, axis=1), weight)
            at = slice(start, start + size)
            keep((xt_z, xt_r, xt_q), at, total, (size, cols, hid), base)

    inner = ((4, rows // 2 - 2), (rows // 2 + 2, rows // 2 - 2))
    outer = ((0, 4), (rows, 4))

    loads[3].wait()
    inputs_lat(0, CTX, biases(1), inner)
    sources = [-2, 2, 4 - 8 * parity]

    def hand_on(number):
        arrived(place(sources[number]))
        forward(number + 1, sources[number]).start()

    receive_lon(CTX, joined)
    hand_on(0)
    hand_on(1)
    inputs_lon(0, biases(0))
    hand_on(2)
    receive_lat(CTX)
    inputs_lat(0, CTX, biases(1), outer)

    scale = chans ** (-0.5)

    def correlate(*spots):
        keys = joined_up([pool[spot] for spot in spots], 0)
        points = pool.shape[1]
        step = rows // 4

        def chunk(index, carry):
            at = pl.ds(index * step, step)
            value = lax.dot_general(
                flat(one_ref[at]), keys, (((1,), (1,)), ((), ())), preferred_element_type=F32
            )
            value = (value * scale).astype(BF)
            for number, spot in enumerate(spots):
                part = value[:, number * points : (number + 1) * points]
                corr[spot, at] = part.reshape(step, cols, points)
            return carry

        lax.fori_loop(0, 4, chunk, 0)

    loads[4].wait()
    correlate(place(0), place(2))
    if n_lon > 2 * RMAX:
        arrived(place(4 * (2 * parity - 1)))
        correlate(place(-4))
    correlate(place(-2), place(4))
    for pair in ((-1, 1), (-3, 3)):
        for steps in pair:
            arrived(place(steps))
        correlate(*[place(steps) for steps in pair])

    loads[5].wait()
    live = count_ref[0, 0]
    spots = []
    for slot in range(slots):
        offset = offset_ref[0, 0, slot]
        spots.append(jnp.where(offset < lowest, offset + n_lon, offset) - lowest)
        weight = proj_ref[class_ref[0, 0, slot]].astype(F32)
        weight = jnp.where(slot < live, weight, 0.0)
        projs[slot * weight.shape[0] : (slot + 1) * weight.shape[0]] = weight.astype(BF)

    def move(start, size):
        pieces = [flat(corr[spot, start : start + size]) for spot in spots]
        total = dot(jnp.concatenate(pieces, axis=1), projs[...])
        moved = jnp.maximum(total, 0.0).reshape(size, cols, hid)
        joined[start : start + size, main] = moved
        ext[MOT, HALO + start : HALO + start + size] = moved.astype(BF)

    move(0, HALO)
    move(rows - HALO, HALO)
    send_lat(MOT)
    for start in range(HALO, rows - HALO, HALO):
        move(start, HALO)
    send_lon(MOT, joined[:, 8:16], joined[:, cols : 8 + cols])
    for steps in evens:
        direct(steps).wait_send()
    for number, source in enumerate([0] + sources):
        forward(number, source).wait_send()
    inputs_lat(1, MOT, None, inner)
    receive_lon(MOT, joined)
    inputs_lon(1, None)
    receive_lat(MOT)
    inputs_lat(1, MOT, None, outer)
    loads[6].wait()
    loads[7].wait()

    def pass_lon(e, blocks):
        count = sum(size for _, size in blocks)

        def take(ref, *rest):
            parts = [ref[(slice(start, start + size),) + rest] for start, size in blocks]
            return joined_up(parts, 0)

        def put(ref, value, *rest, shift=0, lead=()):
            done = 0
            for start, size in blocks:
                at = slice(start + shift, start + shift + size)
                ref[lead + (at,) + rest] = value[done : done + size]
                done += size

        pieces = [flat(take(s_lon, slice(2 + k, 2 + k + near))).astype(BF) for k in range(5)]
        mixed = dot(jnp.concatenate(pieces, axis=1), zr_ref[0])
        shape = (count, near, hid)
        put(z_lon, sigmoid(take(xl_z) + mixed[:, :hid].reshape(shape)))
        reset = sigmoid(take(xl_r) + mixed[:, hid:].reshape(shape))
        put(rs_lon, reset * take(s_lon, slice(4, 4 + near)))
        pieces = [flat(take(rs_lon, slice(2 + k, 2 + k + cols))).astype(BF) for k in range(5)]
        mixed = dot(jnp.concatenate(pieces, axis=1), q_ref[0]).reshape(count, cols, hid)
        middle = slice(4, 4 + cols)
        candidate = jnp.tanh(take(xl_q, middle) + mixed)
        state = take(s_lon, main)
        state = state + take(z_lon, middle) * (candidate - state)
        put(s_lat, state)
        put(ext, state.astype(BF), shift=HALO, lead=(e,))

    def gates_lat(e, blocks, bands):
        wide = sum(band.stop - band.start for band in bands)

        def take(ref, lead, start, size):
            at = slice(start, start + size)
            return joined_up([ref[lead + (at, band)] for band in bands], 1)

        def put(ref, start, size, value):
            done = 0
            for band in bands:
                width = band.stop - band.start
                ref[start : start + size, band] = value[:, done : done + width]
                done += width

        pieces = [
            joined_up([flat(take(ext, (e,), start + k, size)) for start, size in blocks], 0)
            for k in range(5)
        ]
        mixed = dot(jnp.concatenate(pieces, axis=1), zr_ref[1])
        done = 0
        for start, size in blocks:
            shape = (size, wide, hid)
            part = mixed[done : done + size * wide]
            done += size * wide
            z = sigmoid(take(xt_z, (), start, size) + part[:, :hid].reshape(shape))
            put(z_lat, start, size, z)
            reset = sigmoid(take(xt_r, (), start, size) + part[:, hid:].reshape(shape))
            if start == 0:
                held = [take(ext, (e,), 2, 2).astype(F32), take(s_lat, (), 0, 2)]
            elif start + size == rows + 4:
                held = [take(s_lat, (), rows - 2, 2), take(ext, (e,), rows + HALO, 2).astype(F32)]
            else:
                held = [take(s_lat, (), start - 2, size)]
            put(rs_lat, start, size, (reset * joined_up(held, 0)).astype(BF))

    def update_lat(bands):
        wide = sum(band.stop - band.start for band in bands)

        def take(ref, start):
            return joined_up([ref[start : start + rows, band] for band in bands], 1)

        pieces = [flat(take(rs_lat, k)) for k in range(5)]
        mixed = dot(jnp.concatenate(pieces, axis=1), q_ref[1]).reshape(rows, wide, hid)
        candidate = jnp.tanh(take(xt_q, 2) + mixed)
        state = take(s_lat, 0)
        state = state + take(z_lat, 2) * (candidate - state)
        done = 0
        for band in bands:
            width = band.stop - band.start
            s_lon[:, 8 + band.start : 8 + band.stop] = state[:, done : done + width]
            done += width
        return state

    edges = (slice(0, 16), slice(cols - 16, cols))
    centre = (slice(16, cols - 16),)
    panel = (slice(0, cols),)

    def iteration(index, carry):
        e = STATE + index
        receive_lon(e, s_lon)
        pass_lon(e, ((0, HALO), (rows - HALO, HALO)))
        send_lat(e)
        pass_lon(e, ((HALO, rows - 2 * HALO),))
        gates_lat(e, ((4, rows - 4),), panel)
        receive_lat(e)
        gates_lat(e, outer, edges)
        state = update_lat(edges)

        @pl.when(index < ITERS - 1)
        def _():
            send_lon(e + 1, s_lon[:, 8:16], s_lon[:, cols : 8 + cols])

        gates_lat(e, outer, centre)
        update_lat(centre)
        return carry

    lax.fori_loop(0, ITERS, iteration, 0)
    out_ref[...] = s_lon[:, main].astype(BF)


def local(
    n_lat,
    n_lon,
    feat_one,
    feat_two,
    context_in,
    hidden_init,
    corr_proj,
    input_conv,
    state_zr,
    state_q,
    update_bias,
    gate_bias,
    blk_offset,
    blk_class,
    blk_count,
):
    rows, cols, chans = feat_one.shape
    hid = hidden_init.shape[2]
    points = POOLR * POOLC
    slots = blk_offset.shape[2]
    reach = min(n_lon, 2 * RMAX + 1)
    wide, near = cols + 16, cols + 8
    tall = rows + 2 * HALO
    count = STATE + ITERS
    taps = state_zr.shape[1]
    state_zr = state_zr.reshape(2, taps * hid, 2 * hid)
    state_q = state_q.reshape(2, taps * hid, hid)
    vmem = pl.BlockSpec(memory_space=pltpu.VMEM)
    smem = pl.BlockSpec(memory_space=pltpu.SMEM)
    hbm = pl.BlockSpec(memory_space=pl.ANY)
    held = (feat_one, feat_two, hidden_init, corr_proj, input_conv, state_zr, state_q)
    return pl.pallas_call(
        functools.partial(kernel, n_lat, n_lon),
        out_shape=jax.ShapeDtypeStruct((rows, cols, hid), BF),
        in_specs=[smem] * 3 + [hbm] * 8 + [vmem] * 2,
        out_specs=vmem,
        scratch_shapes=[pltpu.VMEM(value.shape, BF) for value in held]
        + [
            pltpu.VMEM((count, tall, cols, hid), BF),
            pltpu.VMEM((count, 2, rows // 2, 16, hid), BF),
            pltpu.VMEM((count, 2, rows // 2, 16, hid), BF),
            pltpu.VMEM((reach, points, chans), BF),
            pltpu.VMEM((reach, rows, cols, points), BF),
            pltpu.VMEM((slots * points, hid), BF),
            pltpu.VMEM((rows, wide, hid), F32),
            pltpu.VMEM((rows, near, hid), F32),
            pltpu.VMEM((rows, near, hid), F32),
            pltpu.VMEM((rows, near, hid), F32),
            pltpu.VMEM((rows + 4, cols, hid), F32),
            pltpu.VMEM((rows + 4, cols, hid), F32),
            pltpu.VMEM((rows + 4, cols, hid), F32),
            pltpu.VMEM((rows, wide, hid), F32),
            pltpu.VMEM((rows, cols, hid), F32),
            pltpu.VMEM((rows, near, hid), F32),
            pltpu.VMEM((rows + 4, cols, hid), BF),
            pltpu.VMEM((rows, near, hid), F32),
            pltpu.VMEM((rows + 4, cols, hid), F32),
            pltpu.SemaphoreType.DMA((8,)),
            pltpu.SemaphoreType.DMA((count, 2)),
            pltpu.SemaphoreType.DMA((count, 2)),
            pltpu.SemaphoreType.DMA((count, 2)),
            pltpu.SemaphoreType.DMA((count, 2)),
            pltpu.SemaphoreType.DMA((4,)),
            pltpu.SemaphoreType.DMA((reach,)),
            pltpu.SemaphoreType.DMA((4,)),
        ],
        compiler_params=pltpu.CompilerParams(
            collective_id=0, has_side_effects=True, vmem_limit_bytes=56 * 1024 * 1024
        ),
        name="refine",
    )(
        blk_offset,
        blk_class,
        blk_count,
        feat_one,
        feat_two,
        context_in,
        hidden_init,
        corr_proj,
        input_conv,
        state_zr,
        state_q,
        update_bias,
        gate_bias,
    )


def solution(mesh):
    placed = (
        P("lat", "lon", None),
        P("lat", "lon", None),
        P("lat", "lon", None),
        P("lat", "lon", None),
        P(),
        P(),
        P(),
        P(),
        P(),
        P(),
        P("lat", "lon", None),
        P("lat", "lon", None),
        P("lat", "lon"),
    )
    return jax.shard_map(
        functools.partial(local, mesh.shape["lat"], mesh.shape["lon"]),
        mesh=mesh,
        in_specs=placed,
        out_specs=P("lat", "lon", None),
        check_vma=False,
    )
```

time: 78.6 us -> 61.9 us (0.79)
  Pallas kernels: 68.9 us -> 59.3 us
  local copies, waits for them, and re-layouts: 8.23 us -> 1.67 us
    pallas_call x1, Pallas kernels: 68.9 us -> 59.3 us  [local(): pl.pallas_call(functools.partial(kernel, n_lat, n_lon), out_shape=jax.Sha...]
    unnamed x19 -> x1, local copies, waits for them, and re-layouts: 8.23 us -> 1.67 us
where the time goes in v2:
time: 61.9 us; the launch traced here: 61.7 us
  Pallas kernels  59.3 us (96%)
  local copies, waits for them, and re-layouts  1.67 us (3%)
  between operations  0.66 us (1%)
    pallas_call x1, Pallas kernels, local(): pl.pallas_call(functools.partial(kernel, n_lat, n_lon), out_shape=jax.Sha...  59.3 us
    unnamed x1, local copies, waits for them, and re-layouts  1.67 us

profile of v2, /device:TPU:0, one launch (start us, length us, event | category | flops | bytes accessed | tf_op | source)
XLA Modules:
  0.0 61.7 jit_solution(7866423228237073572)
XLA Ops:
  0.7 59.3 %refine.1 = bf16[16,64,128]{2,1,0:T(8,128)(2,1)} custom-call(s32[1,1,12]{2,1,0:T(1,128)} %offset_ref.1, s32[1,1,12]{2,1,0:T(1,128)} %class_ref.1, s32[1,1]{1,0:T(1,128)S(6)} %copy.15.count_ref, bf16[16,64,256]{2,1,0:T(8,128)(2,1)} %one_hbm.1, bf16[16,64,256]{2,1,0:T(8,128)(2,1)} %two_hbm.1, bf16[16,64,128]{2,1,0:T(8,128)(2,1)} %ctx_hbm.1, ...), custom_call_target="tpu_custom_call" | custom-call | tf_op jit(solution)/shard_map/refine/pallas_call | solution.py:528
  60.0 1.7 %copy.16 = bf16[16,64,128]{2,1,0:T(8,128)(2,1)} copy(bf16[16,64,128]{2,1,0:T(8,128)(2,1)} %refine.1) | data formatting | bytes 524288

commit v3 on v2

--- a/solution.py
+++ b/solution.py
@@ -146,12 +146,16 @@
     def _():
         pl.semaphore_signal(barrier, inc=1, device_id=(south, lon), device_id_type=MESH)
 
-    def to_lat(e, way):
+    left, right = slice(0, 16), slice(cols - 16, cols)
+    bands = (left, right, slice(16, cols - 16))
+    edges, centre, panel = (0, 1), (2,), (0, 1, 2)
+
+    def to_lat(e, way, band):
         return pltpu.make_async_remote_copy(
-            src_ref=ext.at[e, bottom if way else top],
-            dst_ref=ext.at[e, above if way else below],
-            send_sem=ns_send.at[e, way],
-            recv_sem=ns_recv.at[e, way],
+            src_ref=ext.at[e, bottom if way else top, bands[band]],
+            dst_ref=ext.at[e, above if way else below, bands[band]],
+            send_sem=ns_send.at[e, way, band],
+            recv_sem=ns_recv.at[e, way, band],
             device_id=(south if way else north, lon),
             device_id_type=MESH,
         )
@@ -166,32 +170,33 @@
             device_id_type=MESH,
         )
 
-    def send_lat(e):
+    def send_lat(e, way, chosen=panel):
+        @pl.when(has_s if way else has_n)
+        def _():
+            for band in chosen:
+                to_lat(e, way, band).start()
+
+    def receive_lat(e, chosen=panel):
+        @pl.when(has_s)
+        def _():
+            for band in chosen:
+                to_lat(e, 0, band).wait_recv()
+                to_lat(e, 1, band).wait_send()
+
         @pl.when(has_n)
         def _():
-            to_lat(e, 0).start()
-
-        @pl.when(has_s)
-        def _():
-            to_lat(e, 1).start()
-
-    def receive_lat(e):
-        @pl.when(has_s)
-        def _():
-            to_lat(e, 0).wait_recv()
-            to_lat(e, 1).wait_send()
-
-        @pl.when(jnp.logical_not(has_s))
-        def _():
+            for band in chosen:
+                to_lat(e, 1, band).wait_recv()
+                to_lat(e, 0, band).wait_send()
+
+    @pl.when(jnp.logical_not(has_s))
+    def _():
+        for e in range(ext.shape[0]):
             ext[e, below] = jnp.zeros((HALO, cols, hid), BF)
 
-        @pl.when(has_n)
-        def _():
-            to_lat(e, 1).wait_recv()
-            to_lat(e, 0).wait_send()
-
-        @pl.when(jnp.logical_not(has_n))
-        def _():
+    @pl.when(jnp.logical_not(has_n))
+    def _():
+        for e in range(ext.shape[0]):
             ext[e, above] = jnp.zeros((HALO, cols, hid), BF)
 
     def send_lon(e, low, high):
@@ -255,7 +260,8 @@
         direct(steps).start()
     forward(0, 0).start()
     loads[1].wait()
-    send_lat(CTX)
+    send_lat(CTX, 0)
+    send_lat(CTX, 1)
     whole = ext[CTX, body].astype(F32)
     joined[:, main] = whole
     send_lon(CTX, whole[:, 0:8], whole[:, cols - 8 :])
@@ -359,19 +365,35 @@
         weight = jnp.where(slot < live, weight, 0.0)
         projs[slot * weight.shape[0] : (slot + 1) * weight.shape[0]] = weight.astype(BF)
 
-    def move(start, size):
-        pieces = [flat(corr[spot, start : start + size]) for spot in spots]
-        total = dot(jnp.concatenate(pieces, axis=1), projs[...])
-        moved = jnp.maximum(total, 0.0).reshape(size, cols, hid)
-        joined[start : start + size, main] = moved
-        ext[MOT, HALO + start : HALO + start + size] = moved.astype(BF)
-
-    move(0, HALO)
-    move(rows - HALO, HALO)
-    send_lat(MOT)
-    for start in range(HALO, rows - HALO, HALO):
-        move(start, HALO)
+    def move(chosen):
+        step = rows // 2
+        wide = sum(bands[band].stop - bands[band].start for band in chosen)
+
+        def chunk(index, carry):
+            start = index * step
+            at = pl.ds(start, step)
+            pieces = []
+            for spot in spots:
+                parts = [corr[spot, at, bands[band]] for band in chosen]
+                pieces.append(flat(joined_up(parts, 1)))
+            total = dot(jnp.concatenate(pieces, axis=1), projs[...])
+            moved = jnp.maximum(total, 0.0).reshape(step, wide, hid)
+            done = 0
+            for band in chosen:
+                low, high = bands[band].start, bands[band].stop
+                part = moved[:, done : done + high - low]
+                done += high - low
+                joined[at, 8 + low : 8 + high] = part
+                ext[MOT, pl.ds(HALO + start, step), bands[band]] = part.astype(BF)
+            return carry
+
+        lax.fori_loop(0, 2, chunk, 0)
+
+    move(edges)
     send_lon(MOT, joined[:, 8:16], joined[:, cols : 8 + cols])
+    move(centre)
+    send_lat(MOT, 0)
+    send_lat(MOT, 1)
     for steps in evens:
         direct(steps).wait_send()
     for number, source in enumerate([0] + sources):
@@ -379,8 +401,6 @@
     inputs_lat(1, MOT, None, inner)
     receive_lon(MOT, joined)
     inputs_lon(1, None)
-    receive_lat(MOT)
-    inputs_lat(1, MOT, None, outer)
     loads[6].wait()
     loads[7].wait()
 
@@ -413,16 +433,17 @@
         put(s_lat, state)
         put(ext, state.astype(BF), shift=HALO, lead=(e,))
 
-    def gates_lat(e, blocks, bands):
-        wide = sum(band.stop - band.start for band in bands)
+    def gates_lat(e, blocks, chosen):
+        spans = (slice(0, cols),) if chosen is panel else [bands[band] for band in chosen]
+        wide = sum(band.stop - band.start for band in spans)
 
         def take(ref, lead, start, size):
             at = slice(start, start + size)
-            return joined_up([ref[lead + (at, band)] for band in bands], 1)
+            return joined_up([ref[lead + (at, band)] for band in spans], 1)
 
         def put(ref, start, size, value):
             done = 0
-            for band in bands:
+            for band in spans:
                 width = band.stop - band.start
                 ref[start : start + size, band] = value[:, done : done + width]
                 done += width
@@ -448,11 +469,12 @@
                 held = [take(s_lat, (), start - 2, size)]
             put(rs_lat, start, size, (reset * joined_up(held, 0)).astype(BF))
 
-    def update_lat(bands):
-        wide = sum(band.stop - band.start for band in bands)
+    def update_lat(chosen):
+        spans = [bands[band] for band in chosen]
+        wide = sum(band.stop - band.start for band in spans)
 
         def take(ref, start):
-            return joined_up([ref[start : start + rows, band] for band in bands], 1)
+            return joined_up([ref[start : start + rows, band] for band in spans], 1)
 
         pieces = [flat(take(rs_lat, k)) for k in range(5)]
         mixed = dot(jnp.concatenate(pieces, axis=1), q_ref[1]).reshape(rows, wide, hid)
@@ -460,31 +482,37 @@
         state = take(s_lat, 0)
         state = state + take(z_lat, 2) * (candidate - state)
         done = 0
-        for band in bands:
+        for band in spans:
             width = band.stop - band.start
             s_lon[:, 8 + band.start : 8 + band.stop] = state[:, done : done + width]
             done += width
-        return state
-
-    edges = (slice(0, 16), slice(cols - 16, cols))
-    centre = (slice(16, cols - 16),)
-    panel = (slice(0, cols),)
 
     def iteration(index, carry):
         e = STATE + index
         receive_lon(e, s_lon)
-        pass_lon(e, ((0, HALO), (rows - HALO, HALO)))
-        send_lat(e)
+        pass_lon(e, ((0, HALO),))
+        send_lat(e, 0, edges)
+        pass_lon(e, ((rows - HALO, HALO),))
+        send_lat(e, 1, edges)
+        send_lat(e, 0, centre)
+        send_lat(e, 1, centre)
+
+        @pl.when(index == 0)
+        def _():
+            receive_lat(MOT)
+            inputs_lat(1, MOT, None, outer)
+
         pass_lon(e, ((HALO, rows - 2 * HALO),))
         gates_lat(e, ((4, rows - 4),), panel)
-        receive_lat(e)
+        receive_lat(e, edges)
         gates_lat(e, outer, edges)
-        state = update_lat(edges)
+        update_lat(edges)
 
         @pl.when(index < ITERS - 1)
         def _():
             send_lon(e + 1, s_lon[:, 8:16], s_lon[:, cols : 8 + cols])
 
+        receive_lat(e, centre)
         gates_lat(e, outer, centre)
         update_lat(centre)
         return carry
@@ -552,8 +580,8 @@
             pltpu.VMEM((rows, near, hid), F32),
             pltpu.VMEM((rows + 4, cols, hid), F32),
             pltpu.SemaphoreType.DMA((8,)),
-            pltpu.SemaphoreType.DMA((count, 2)),
-            pltpu.SemaphoreType.DMA((count, 2)),
+            pltpu.SemaphoreType.DMA((count, 2, 3)),
+            pltpu.SemaphoreType.DMA((count, 2, 3)),
             pltpu.SemaphoreType.DMA((count, 2)),
             pltpu.SemaphoreType.DMA((count, 2)),
             pltpu.SemaphoreType.DMA((4,)),

time: 61.9 us -> 57.6 us (0.931)
  Pallas kernels: 59.3 us -> 55.1 us
    pallas_call x1, Pallas kernels: 59.3 us -> 55.1 us  [local(): pl.pallas_call(functools.partial(kernel, n_lat, n_lon), out_shape=jax.Sha...]
where the time goes in v3:
time: 57.6 us; the launch traced here: 57.5 us
  Pallas kernels  55.1 us (96%)
  local copies, waits for them, and re-layouts  1.67 us (3%)
  between operations  0.66 us (1%)
    pallas_call x1, Pallas kernels, local(): pl.pallas_call(functools.partial(kernel, n_lat, n_lon), out_shape=jax.Sha...  55.1 us
    unnamed x1, local copies, waits for them, and re-layouts  1.67 us

profile of v3, /device:TPU:0, one launch (start us, length us, event | category | flops | bytes accessed | tf_op | source)
XLA Modules:
  0.0 57.5 jit_solution(14479388010282983988)
XLA Ops:
  0.7 55.1 %refine.1 = bf16[16,64,128]{2,1,0:T(8,128)(2,1)} custom-call(s32[1,1,12]{2,1,0:T(1,128)} %offset_ref.1, s32[1,1,12]{2,1,0:T(1,128)} %class_ref.1, s32[1,1]{1,0:T(1,128)S(6)} %copy.15.count_ref, bf16[16,64,256]{2,1,0:T(8,128)(2,1)} %one_hbm.1, bf16[16,64,256]{2,1,0:T(8,128)(2,1)} %two_hbm.1, bf16[16,64,128]{2,1,0:T(8,128)(2,1)} %ctx_hbm.1, ...), custom_call_target="tpu_custom_call" | custom-call | tf_op jit(solution)/shard_map/refine/pallas_call | solution.py:556
  55.8 1.7 %copy.16 = bf16[16,64,128]{2,1,0:T(8,128)(2,1)} copy(bf16[16,64,128]{2,1,0:T(8,128)(2,1)} %refine.1) | data formatting | bytes 524288

commit v4 on v3

--- a/solution.py
+++ b/solution.py
@@ -59,12 +59,11 @@
     zr_ref,
     q_ref,
     ext,
-    side_out,
-    side_in,
+    turned,
     pool,
     corr,
     projs,
-    joined,
+    turn,
     xl_z,
     xl_r,
     xl_q,
@@ -88,7 +87,7 @@
 ):
     rows, cols, chans = one_ref.shape
     hid = init_ref.shape[2]
-    near = cols + 8
+    near = cols + 4
     slots = offset_ref.shape[2]
     lat, lon = lax.axis_index("lat"), lax.axis_index("lon")
     north, south = lax.rem(lat + n_lat - 1, n_lat), lax.rem(lat + 1, n_lat)
@@ -103,7 +102,6 @@
     above = slice(0, HALO)
     below = slice(rows + HALO, rows + 2 * HALO)
     body = slice(HALO, HALO + rows)
-    main = slice(8, 8 + cols)
 
     loads = [
         pltpu.make_async_copy(source, target, load_sem.at[number])
@@ -162,8 +160,8 @@
 
     def to_lon(e, way):
         return pltpu.make_async_remote_copy(
-            src_ref=side_out.at[e, way],
-            dst_ref=side_in.at[e, 1 - way],
+            src_ref=turned.at[e, cols : cols + HALO] if way else turned.at[e, HALO : 2 * HALO],
+            dst_ref=turned.at[e, 0:HALO] if way else turned.at[e, cols + HALO :],
             send_sem=ew_send.at[e, way],
             recv_sem=ew_recv.at[e, way],
             device_id=(lat, east if way else west),
@@ -199,17 +197,23 @@
         for e in range(ext.shape[0]):
             ext[e, above] = jnp.zeros((HALO, cols, hid), BF)
 
-    def send_lon(e, low, high):
-        for way, value in enumerate((low, high)):
-            side_out[e, way] = value.reshape(rows // 2, 16, hid).astype(BF)
+    def send_lon(e):
         for way in range(2):
             to_lon(e, way).start()
 
-    def receive_lon(e, target):
+    def receive_lon(e):
         for way in range(2):
             to_lon(e, way).wait()
-        target[:, 0:8] = side_in[e, 0].astype(F32).reshape(rows, 8, hid)
-        target[:, 8 + cols :] = side_in[e, 1].astype(F32).reshape(rows, 8, hid)
+
+    def turn_rows(value, band, target, first=0):
+        low, high = band.start, band.stop
+        for row in range(value.shape[0]):
+            target[pl.ds(low * rows + first + row, high - low, stride=rows), :] = value[row]
+
+    def cast_columns(source, band, e):
+        low, high = band.start, band.stop
+        value = source[low * rows : high * rows, :].astype(BF).reshape(high - low, rows, hid)
+        turned[e, HALO + low : HALO + high] = value
 
     def direct(steps):
         return pltpu.make_async_remote_copy(
@@ -262,13 +266,14 @@
     loads[1].wait()
     send_lat(CTX, 0)
     send_lat(CTX, 1)
-    whole = ext[CTX, body].astype(F32)
-    joined[:, main] = whole
-    send_lon(CTX, whole[:, 0:8], whole[:, cols - 8 :])
+    every = slice(0, cols)
+    turn_rows(ext[CTX, body].astype(F32), every, turn)
+    cast_columns(turn, every, CTX)
+    send_lon(CTX)
     loads[2].wait()
-    whole = init_ref[...].astype(F32)
-    s_lon[:, main] = whole
-    send_lon(STATE, whole[:, 0:8], whole[:, cols - 8 :])
+    turn_rows(init_ref[...].astype(F32), every, s_lon)
+    cast_columns(s_lon, every, STATE)
+    send_lon(STATE)
 
     def weights(index, part):
         channels = slice(part * hid, (part + 1) * hid)
@@ -284,15 +289,15 @@
             value = total[:, number * hid : (number + 1) * hid].reshape(shape)
             store[at] = value + (store[at] if base is None else base[number])
 
-    def inputs_lon(part, base):
+    def inputs_lon(part, e, base):
         weight = weights(0, part)
-        step = rows // 2
+        step = near // 2
 
         def chunk(index, carry):
-            at = pl.ds(index * step, step)
-            pieces = [flat(joined[at, 2 + k : 2 + k + near]).astype(BF) for k in range(5)]
+            start = index * step
+            pieces = [flat(turned[e, pl.ds(start + k, step)]) for k in range(5)]
             total = dot(jnp.concatenate(pieces, axis=1), weight)
-            keep((xl_z, xl_r, xl_q), at, total, (step, near, hid), base)
+            keep((xl_z, xl_r, xl_q), pl.ds(start, step), total, (step, rows, hid), base)
             return carry
 
         lax.fori_loop(0, 2, chunk, 0)
@@ -316,10 +321,10 @@
         arrived(place(sources[number]))
         forward(number + 1, sources[number]).start()
 
-    receive_lon(CTX, joined)
+    receive_lon(CTX)
     hand_on(0)
     hand_on(1)
-    inputs_lon(0, biases(0))
+    inputs_lon(0, CTX, biases(0))
     hand_on(2)
     receive_lat(CTX)
     inputs_lat(0, CTX, biases(1), outer)
@@ -369,9 +374,8 @@
         step = rows // 2
         wide = sum(bands[band].stop - bands[band].start for band in chosen)
 
-        def chunk(index, carry):
-            start = index * step
-            at = pl.ds(start, step)
+        for start in range(0, rows, step):
+            at = slice(start, start + step)
             pieces = []
             for spot in spots:
                 parts = [corr[spot, at, bands[band]] for band in chosen]
@@ -383,14 +387,13 @@
                 low, high = bands[band].start, bands[band].stop
                 part = moved[:, done : done + high - low]
                 done += high - low
-                joined[at, 8 + low : 8 + high] = part
-                ext[MOT, pl.ds(HALO + start, step), bands[band]] = part.astype(BF)
-            return carry
-
-        lax.fori_loop(0, 2, chunk, 0)
+                turn_rows(part, bands[band], turn, start)
+                ext[MOT, HALO + start : HALO + start + step, bands[band]] = part.astype(BF)
+        for band in chosen:
+            cast_columns(turn, bands[band], MOT)
 
     move(edges)
-    send_lon(MOT, joined[:, 8:16], joined[:, cols : 8 + cols])
+    send_lon(MOT)
     move(centre)
     send_lat(MOT, 0)
     send_lat(MOT, 1)
@@ -399,39 +402,64 @@
     for number, source in enumerate([0] + sources):
         forward(number, source).wait_send()
     inputs_lat(1, MOT, None, inner)
-    receive_lon(MOT, joined)
-    inputs_lon(1, None)
+    receive_lon(MOT)
+    inputs_lon(1, MOT, None)
     loads[6].wait()
     loads[7].wait()
 
-    def pass_lon(e, blocks):
-        count = sum(size for _, size in blocks)
-
-        def take(ref, *rest):
-            parts = [ref[(slice(start, start + size),) + rest] for start, size in blocks]
-            return joined_up(parts, 0)
-
-        def put(ref, value, *rest, shift=0, lead=()):
-            done = 0
-            for start, size in blocks:
-                at = slice(start + shift, start + shift + size)
-                ref[lead + (at,) + rest] = value[done : done + size]
-                done += size
-
-        pieces = [flat(take(s_lon, slice(2 + k, 2 + k + near))).astype(BF) for k in range(5)]
+    def gates_lon(e, blocks):
+        pieces = [
+            joined_up([flat(turned[e, start + k : start + k + size]) for start, size in blocks], 0)
+            for k in range(5)
+        ]
         mixed = dot(jnp.concatenate(pieces, axis=1), zr_ref[0])
-        shape = (count, near, hid)
-        put(z_lon, sigmoid(take(xl_z) + mixed[:, :hid].reshape(shape)))
-        reset = sigmoid(take(xl_r) + mixed[:, hid:].reshape(shape))
-        put(rs_lon, reset * take(s_lon, slice(4, 4 + near)))
-        pieces = [flat(take(rs_lon, slice(2 + k, 2 + k + cols))).astype(BF) for k in range(5)]
-        mixed = dot(jnp.concatenate(pieces, axis=1), q_ref[0]).reshape(count, cols, hid)
-        middle = slice(4, 4 + cols)
-        candidate = jnp.tanh(take(xl_q, middle) + mixed)
-        state = take(s_lon, main)
-        state = state + take(z_lon, middle) * (candidate - state)
-        put(s_lat, state)
-        put(ext, state.astype(BF), shift=HALO, lead=(e,))
+        done = 0
+        for start, size in blocks:
+            at = slice(start, start + size)
+            shape = (size, rows, hid)
+            part = mixed[done : done + size * rows]
+            done += size * rows
+            z_lon[at] = sigmoid(xl_z[at] + part[:, :hid].reshape(shape))
+            reset = sigmoid(xl_r[at] + part[:, hid:].reshape(shape))
+            low, high = max(start, 2), min(start + size, cols + 2)
+            held = []
+            if start < 2:
+                held.append(turned[e, 2:HALO].astype(F32))
+            held.append(s_lon[(low - 2) * rows : (high - 2) * rows, :].reshape(-1, rows, hid))
+            if start + size > cols + 2:
+                held.append(turned[e, cols + HALO : cols + HALO + 2].astype(F32))
+            rs_lon[at] = (reset * joined_up(held, 0)).astype(BF)
+
+    def update_lon(e, chosen):
+        spans = [bands[band] for band in chosen]
+
+        def take(ref, shift):
+            parts = [ref[span.start + shift : span.stop + shift] for span in spans]
+            return flat(joined_up(parts, 0))
+
+        pieces = [take(rs_lon, k) for k in range(5)]
+        mixed = dot(jnp.concatenate(pieces, axis=1), q_ref[0])
+        candidate = jnp.tanh(take(xl_q, 2) + mixed)
+        state = joined_up([s_lon[span.start * rows : span.stop * rows, :] for span in spans], 0)
+        state = state + take(z_lon, 2) * (candidate - state)
+        done = 0
+        for span in spans:
+            for column in range(span.start, span.stop):
+                part = state[done * rows : (done + 1) * rows]
+                s_lat[pl.ds(column, rows, stride=cols), :] = part
+                done += 1
+        for span in spans:
+            for row in range(rows):
+                part = s_lat[row * cols + span.start : row * cols + span.stop, :]
+                ext[e, HALO + row, span] = part.astype(BF)
+
+    def state_rows(spans, start, size):
+        parts = [
+            s_lat[row * cols + span.start : row * cols + span.stop, :]
+            for row in range(start, start + size)
+            for span in spans
+        ]
+        return joined_up(parts, 0).reshape(size, -1, hid)
 
     def gates_lat(e, blocks, chosen):
         spans = (slice(0, cols),) if chosen is panel else [bands[band] for band in chosen]
@@ -462,14 +490,14 @@
             put(z_lat, start, size, z)
             reset = sigmoid(take(xt_r, (), start, size) + part[:, hid:].reshape(shape))
             if start == 0:
-                held = [take(ext, (e,), 2, 2).astype(F32), take(s_lat, (), 0, 2)]
+                held = [take(ext, (e,), 2, 2).astype(F32), state_rows(spans, 0, 2)]
             elif start + size == rows + 4:
-                held = [take(s_lat, (), rows - 2, 2), take(ext, (e,), rows + HALO, 2).astype(F32)]
+                held = [state_rows(spans, rows - 2, 2), take(ext, (e,), rows + HALO, 2).astype(F32)]
             else:
-                held = [take(s_lat, (), start - 2, size)]
+                held = [state_rows(spans, start - 2, size)]
             put(rs_lat, start, size, (reset * joined_up(held, 0)).astype(BF))
 
-    def update_lat(chosen):
+    def update_lat(e, chosen):
         spans = [bands[band] for band in chosen]
         wide = sum(band.stop - band.start for band in spans)
 
@@ -479,21 +507,26 @@
         pieces = [flat(take(rs_lat, k)) for k in range(5)]
         mixed = dot(jnp.concatenate(pieces, axis=1), q_ref[1]).reshape(rows, wide, hid)
         candidate = jnp.tanh(take(xt_q, 2) + mixed)
-        state = take(s_lat, 0)
+        state = state_rows(spans, 0, rows)
         state = state + take(z_lat, 2) * (candidate - state)
         done = 0
         for band in spans:
             width = band.stop - band.start
-            s_lon[:, 8 + band.start : 8 + band.stop] = state[:, done : done + width]
+            part = state[:, done : done + width]
+            out_ref[:, band] = part
+            turn_rows(part, band, s_lon)
+            cast_columns(s_lon, band, e + 1)
             done += width
 
     def iteration(index, carry):
         e = STATE + index
-        receive_lon(e, s_lon)
-        pass_lon(e, ((0, HALO),))
+        gates_lon(e, ((4, cols - 4),))
+        receive_lon(e)
+        gates_lon(e, ((0, 4), (cols, 4)))
+        update_lon(e, edges)
         send_lat(e, 0, edges)
-        pass_lon(e, ((rows - HALO, HALO),))
         send_lat(e, 1, edges)
+        update_lon(e, centre)
         send_lat(e, 0, centre)
         send_lat(e, 1, centre)
 
@@ -502,23 +535,21 @@
             receive_lat(MOT)
             inputs_lat(1, MOT, None, outer)
 
-        pass_lon(e, ((HALO, rows - 2 * HALO),))
         gates_lat(e, ((4, rows - 4),), panel)
         receive_lat(e, edges)
         gates_lat(e, outer, edges)
-        update_lat(edges)
+        update_lat(e, edges)
 
         @pl.when(index < ITERS - 1)
         def _():
-            send_lon(e + 1, s_lon[:, 8:16], s_lon[:, cols : 8 + cols])
+            send_lon(e + 1)
 
         receive_lat(e, centre)
         gates_lat(e, outer, centre)
-        update_lat(centre)
+        update_lat(e, centre)
         return carry
 
     lax.fori_loop(0, ITERS, iteration, 0)
-    out_ref[...] = s_lon[:, main].astype(BF)
 
 
 def local(
@@ -543,7 +574,7 @@
     points = POOLR * POOLC
     slots = blk_offset.shape[2]
     reach = min(n_lon, 2 * RMAX + 1)
-    wide, near = cols + 16, cols + 8
+    near = cols + 4
     tall = rows + 2 * HALO
     count = STATE + ITERS
     taps = state_zr.shape[1]
@@ -553,31 +584,30 @@
     smem = pl.BlockSpec(memory_space=pltpu.SMEM)
     hbm = pl.BlockSpec(memory_space=pl.ANY)
     held = (feat_one, feat_two, hidden_init, corr_proj, input_conv, state_zr, state_q)
-    return pl.pallas_call(
+    hidden = pl.pallas_call(
         functools.partial(kernel, n_lat, n_lon),
-        out_shape=jax.ShapeDtypeStruct((rows, cols, hid), BF),
+        out_shape=jax.ShapeDtypeStruct((rows, cols, hid), F32),
         in_specs=[smem] * 3 + [hbm] * 8 + [vmem] * 2,
         out_specs=vmem,
         scratch_shapes=[pltpu.VMEM(value.shape, BF) for value in held]
         + [
             pltpu.VMEM((count, tall, cols, hid), BF),
-            pltpu.VMEM((count, 2, rows // 2, 16, hid), BF),
-            pltpu.VMEM((count, 2, rows // 2, 16, hid), BF),
+            pltpu.VMEM((count + 1, cols + 2 * HALO, rows, hid), BF),
             pltpu.VMEM((reach, points, chans), BF),
             pltpu.VMEM((reach, rows, cols, points), BF),
             pltpu.VMEM((slots * points, hid), BF),
-            pltpu.VMEM((rows, wide, hid), F32),
-            pltpu.VMEM((rows, near, hid), F32),
-            pltpu.VMEM((rows, near, hid), F32),
-            pltpu.VMEM((rows, near, hid), F32),
+            pltpu.VMEM((cols * rows, hid), F32),
+            pltpu.VMEM((near, rows, hid), F32),
+            pltpu.VMEM((near, rows, hid), F32),
+            pltpu.VMEM((near, rows, hid), F32),
             pltpu.VMEM((rows + 4, cols, hid), F32),
             pltpu.VMEM((rows + 4, cols, hid), F32),
             pltpu.VMEM((rows + 4, cols, hid), F32),
-            pltpu.VMEM((rows, wide, hid), F32),
-            pltpu.VMEM((rows, cols, hid), F32),
-            pltpu.VMEM((rows, near, hid), F32),
+            pltpu.VMEM((cols * rows, hid), F32),
+            pltpu.VMEM((rows * cols, hid), F32),
+            pltpu.VMEM((near, rows, hid), BF),
             pltpu.VMEM((rows + 4, cols, hid), BF),
-            pltpu.VMEM((rows, near, hid), F32),
+            pltpu.VMEM((near, rows, hid), F32),
             pltpu.VMEM((rows + 4, cols, hid), F32),
             pltpu.SemaphoreType.DMA((8,)),
             pltpu.SemaphoreType.DMA((count, 2, 3)),
@@ -607,6 +637,7 @@
         update_bias,
         gate_bias,
     )
+    return hidden.astype(BF)
 
 
 def solution(mesh):

time: 57.6 us -> 57.6 us (level)
  other arithmetic: 0 us -> 1.79 us
  local copies, waits for them, and re-layouts: 1.67 us -> 0 us
    convert_element_type x0 -> x1, other arithmetic: none -> 1.79 us  [local(): return hidden.astype(BF)]
    unnamed x1 -> x0, local copies, waits for them, and re-layouts: 1.67 us -> none
where the time goes in v4:
time: 57.6 us; the launch traced here: 57.4 us
  Pallas kernels  55 us (95%)
  other arithmetic  1.79 us (3%)
  between operations  0.66 us (1%)
    pallas_call x1, Pallas kernels, local(): pl.pallas_call(functools.partial(kernel, n_lat, n_lon), out_shape=jax.Sha...  55 us
    convert_element_type x1, other arithmetic, local(): return hidden.astype(BF)  1.79 us

profile of v4, /device:TPU:0, one launch (start us, length us, event | category | flops | bytes accessed | tf_op | source)
XLA Modules:
  0.0 57.4 jit_solution(10977255441726950875)
XLA Ops:
  0.7 55.0 %refine.1 = f32[16,64,128]{2,1,0:T(8,128)} custom-call(s32[1,1,12]{2,1,0:T(1,128)} %offset_ref.1, s32[1,1,12]{2,1,0:T(1,128)} %class_ref.1, s32[1,1]{1,0:T(1,128)S(6)} %copy.14.count_ref, bf16[16,64,256]{2,1,0:T(8,128)(2,1)} %one_hbm.1, bf16[16,64,256]{2,1,0:T(8,128)(2,1)} %two_hbm.1, bf16[16,64,128]{2,1,0:T(8,128)(2,1)} %ctx_hbm.1, ...), custom_call_target="tpu_custom_call" | custom-call | tf_op jit(solution)/shard_map/refine/pallas_call | solution.py:587
  55.6 1.8 %convert_element_type.3 = bf16[16,64,128]{2,1,0:T(8,128)(2,1)} convert(f32[16,64,128]{2,1,0:T(8,128)} %refine.1) | non-fusion elementwise | flops 131072 | bytes 786432 | tf_op jit(solution)/shard_map/convert_element_type | solution.py:640

commit v5 on v4

--- a/solution.py
+++ b/solution.py
@@ -497,26 +497,40 @@
                 held = [state_rows(spans, start - 2, size)]
             put(rs_lat, start, size, (reset * joined_up(held, 0)).astype(BF))
 
-    def update_lat(e, chosen):
-        spans = [bands[band] for band in chosen]
-        wide = sum(band.stop - band.start for band in spans)
-
-        def take(ref, start):
-            return joined_up([ref[start : start + rows, band] for band in spans], 1)
-
-        pieces = [flat(take(rs_lat, k)) for k in range(5)]
-        mixed = dot(jnp.concatenate(pieces, axis=1), q_ref[1]).reshape(rows, wide, hid)
-        candidate = jnp.tanh(take(xt_q, 2) + mixed)
-        state = state_rows(spans, 0, rows)
-        state = state + take(z_lat, 2) * (candidate - state)
+    def update_lat(e, chosen, blocks):
+        spans = (slice(0, cols),) if chosen is panel else [bands[band] for band in chosen]
+        wide = sum(span.stop - span.start for span in spans)
+
+        def take(ref, start, size):
+            return joined_up([ref[start : start + size, span] for span in spans], 1)
+
+        def rows_of(ref, shift):
+            parts = [flat(take(ref, start + shift, size)) for start, size in blocks]
+            return joined_up(parts, 0)
+
+        pieces = [rows_of(rs_lat, k) for k in range(5)]
+        mixed = dot(jnp.concatenate(pieces, axis=1), q_ref[1])
         done = 0
-        for band in spans:
-            width = band.stop - band.start
-            part = state[:, done : done + width]
-            out_ref[:, band] = part
-            turn_rows(part, band, s_lon)
-            cast_columns(s_lon, band, e + 1)
-            done += width
+        for start, size in blocks:
+            shape = (size, wide, hid)
+            part = mixed[done : done + size * wide].reshape(shape)
+            done += size * wide
+            candidate = jnp.tanh(take(xt_q, start + 2, size) + part)
+            state = state_rows(spans, start, size)
+            state = state + take(z_lat, start + 2, size) * (candidate - state)
+            column = 0
+            for span in spans:
+                width = span.stop - span.start
+                value = state[:, column : column + width]
+                out_ref[start : start + size, span] = value
+                turn_rows(value, span, s_lon, start)
+                column += width
+
+    def cast_bands(e, chosen):
+        for band in chosen:
+            cast_columns(s_lon, bands[band], e)
+
+    rim = ((0, HALO), (rows - HALO, HALO))
 
     def iteration(index, carry):
         e = STATE + index
@@ -536,9 +550,11 @@
             inputs_lat(1, MOT, None, outer)
 
         gates_lat(e, ((4, rows - 4),), panel)
+        update_lat(e, panel, ((HALO, rows - 2 * HALO),))
         receive_lat(e, edges)
         gates_lat(e, outer, edges)
-        update_lat(e, edges)
+        update_lat(e, edges, rim)
+        cast_bands(e + 1, edges)
 
         @pl.when(index < ITERS - 1)
         def _():
@@ -546,7 +562,8 @@
 
         receive_lat(e, centre)
         gates_lat(e, outer, centre)
-        update_lat(e, centre)
+        update_lat(e, centre, rim)
+        cast_bands(e + 1, centre)
         return carry
 
     lax.fori_loop(0, ITERS, iteration, 0)

time: 57.6 us -> 56.5 us (0.981)
  Pallas kernels: 55 us -> 53.9 us
    pallas_call x1, Pallas kernels: 55 us -> 53.9 us  [local(): pl.pallas_call(functools.partial(kernel, n_lat, n_lon), out_shape=jax.Sha...]
where the time goes in v5:
time: 56.5 us; the launch traced here: 56.3 us
  Pallas kernels  53.9 us (95%)
  other arithmetic  1.79 us (3%)
  between operations  0.66 us (1%)
    pallas_call x1, Pallas kernels, local(): pl.pallas_call(functools.partial(kernel, n_lat, n_lon), out_shape=jax.Sha...  53.9 us
    convert_element_type x1, other arithmetic, local(): return hidden.astype(BF)  1.79 us

profile of v5, /device:TPU:0, one launch (start us, length us, event | category | flops | bytes accessed | tf_op | source)
XLA Modules:
  0.0 56.3 jit_solution(8158333722939351148)
XLA Ops:
  0.7 53.9 %refine.1 = f32[16,64,128]{2,1,0:T(8,128)} custom-call(s32[1,1,12]{2,1,0:T(1,128)} %offset_ref.1, s32[1,1,12]{2,1,0:T(1,128)} %class_ref.1, s32[1,1]{1,0:T(1,128)S(6)} %copy.14.count_ref, bf16[16,64,256]{2,1,0:T(8,128)(2,1)} %one_hbm.1, bf16[16,64,256]{2,1,0:T(8,128)(2,1)} %two_hbm.1, bf16[16,64,128]{2,1,0:T(8,128)(2,1)} %ctx_hbm.1, ...), custom_call_target="tpu_custom_call" | custom-call | tf_op jit(solution)/shard_map/refine/pallas_call | solution.py:604
  54.5 1.8 %convert_element_type.3 = bf16[16,64,128]{2,1,0:T(8,128)(2,1)} convert(f32[16,64,128]{2,1,0:T(8,128)} %refine.1) | non-fusion elementwise | flops 131072 | bytes 786432 | tf_op jit(solution)/shard_map/convert_element_type | solution.py:657

commit v6 on v5

--- a/solution.py
+++ b/solution.py
@@ -430,9 +430,7 @@
                 held.append(turned[e, cols + HALO : cols + HALO + 2].astype(F32))
             rs_lon[at] = (reset * joined_up(held, 0)).astype(BF)
 
-    def update_lon(e, chosen):
-        spans = [bands[band] for band in chosen]
-
+    def update_lon(spans):
         def take(ref, shift):
             parts = [ref[span.start + shift : span.stop + shift] for span in spans]
             return flat(joined_up(parts, 0))
@@ -448,7 +446,10 @@
                 part = state[done * rows : (done + 1) * rows]
                 s_lat[pl.ds(column, rows, stride=cols), :] = part
                 done += 1
-        for span in spans:
+
+    def cast_rows(e, chosen):
+        for band in chosen:
+            span = bands[band]
             for row in range(rows):
                 part = s_lat[row * cols + span.start : row * cols + span.stop, :]
                 ext[e, HALO + row, span] = part.astype(BF)
@@ -535,14 +536,16 @@
     def iteration(index, carry):
         e = STATE + index
         gates_lon(e, ((4, cols - 4),))
+        update_lon([slice(HALO, cols - HALO)])
+        cast_rows(e, centre)
+        send_lat(e, 0, centre)
+        send_lat(e, 1, centre)
         receive_lon(e)
         gates_lon(e, ((0, 4), (cols, 4)))
-        update_lon(e, edges)
+        update_lon([slice(0, HALO), slice(cols - HALO, cols)])
+        cast_rows(e, edges)
         send_lat(e, 0, edges)
         send_lat(e, 1, edges)
-        update_lon(e, centre)
-        send_lat(e, 0, centre)
-        send_lat(e, 1, centre)
 
         @pl.when(index == 0)
         def _():

time: 56.5 us -> 57.4 us (1.016)
  Pallas kernels: 53.9 us -> 54.7 us
    pallas_call x1, Pallas kernels: 53.9 us -> 54.7 us  [local(): pl.pallas_call(functools.partial(kernel, n_lat, n_lon), out_shape=jax.Sha...]
where the time goes in v6:
time: 57.4 us; the launch traced here: 57.2 us
  Pallas kernels  54.7 us (95%)
  other arithmetic  1.79 us (3%)
  between operations  0.66 us (1%)
    pallas_call x1, Pallas kernels, local(): pl.pallas_call(functools.partial(kernel, n_lat, n_lon), out_shape=jax.Sha...  54.7 us
    convert_element_type x1, other arithmetic, local(): return hidden.astype(BF)  1.79 us

profile of v6, /device:TPU:0, one launch (start us, length us, event | category | flops | bytes accessed | tf_op | source)
XLA Modules:
  0.0 57.2 jit_solution(2972363263400331939)
XLA Ops:
  0.7 54.7 %refine.1 = f32[16,64,128]{2,1,0:T(8,128)} custom-call(s32[1,1,12]{2,1,0:T(1,128)} %offset_ref.1, s32[1,1,12]{2,1,0:T(1,128)} %class_ref.1, s32[1,1]{1,0:T(1,128)S(6)} %copy.14.count_ref, bf16[16,64,256]{2,1,0:T(8,128)(2,1)} %one_hbm.1, bf16[16,64,256]{2,1,0:T(8,128)(2,1)} %two_hbm.1, bf16[16,64,128]{2,1,0:T(8,128)(2,1)} %ctx_hbm.1, ...), custom_call_target="tpu_custom_call" | custom-call | tf_op jit(solution)/shard_map/refine/pallas_call | solution.py:607
  55.4 1.8 %convert_element_type.3 = bf16[16,64,128]{2,1,0:T(8,128)(2,1)} convert(f32[16,64,128]{2,1,0:T(8,128)} %refine.1) | non-fusion elementwise | flops 131072 | bytes 786432 | tf_op jit(solution)/shard_map/convert_element_type | solution.py:660
